TPU v7x, 128 devices: a whole 4x4x4 slice. The times are simulated.
128 devices in a mesh: grp: 16 (over x_hi, z, core), tp: 8 (over x_lo, y).
Axes of the slice: x: 4 (x_hi: 2, x_lo: 2; x = x_hi * 2 + x_lo), y: 4, z: 4, core: 2. Of those that a mesh axis runs over, the one named last changes fastest.
Arguments:
- hidden: bfloat16 [14336, 14336], P('grp', 'tp'), may hold values from -6 to 6
- frozen_down_matrix: bfloat16 [14336, 4096], P('tp'), may hold values from -0.046875 to 0.046875
- cotangent: bfloat16 [14336, 4096], P('grp', 'tp'), may hold values from -6 to 6
- adapter_input_maps: float32 [16, 64, 14336], P('grp', None, 'tp'), may hold values from -0.046875 to 0.046875
- adapter_output_maps: float32 [16, 64, 4096], P('grp', None, 'tp'), may hold values from -0.3 to 0.3
- input_first_moment: float32 [16, 64, 14336], P('grp', None, 'tp'), may hold values from -0.06 to 0.06
- input_second_moment: float32 [16, 64, 14336], P('grp', None, 'tp'), may hold values from 1e-06 to 0.0001
- output_first_moment: float32 [16, 64, 4096], P('grp', None, 'tp'), may hold values from -0.024 to 0.024
- output_second_moment: float32 [16, 64, 4096], P('grp', None, 'tp'), may hold values from 1e-07 to 1e-05
- group_adapter_list: int32 [16, 4], P('grp'), may hold values from 0 to 15, all different within a row
- token_adapter_slot: int32 [14336], P('grp'), may hold values from -1 to 3, as said below
Outputs:
- output: bfloat16 [14336, 4096], P('grp', 'tp')
- hidden_gradient: bfloat16 [14336, 14336], P('grp', 'tp')
- updated_input_maps: float32 [16, 64, 14336], P('grp', None, 'tp')
- updated_output_maps: float32 [16, 64, 4096], P('grp', None, 'tp')
- updated_input_first_moment: float32 [16, 64, 14336], P('grp', None, 'tp')
- updated_input_second_moment: float32 [16, 64, 14336], P('grp', None, 'tp')
- updated_output_first_moment: float32 [16, 64, 4096], P('grp', None, 'tp')
- updated_output_second_moment: float32 [16, 64, 4096], P('grp', None, 'tp')
Inputs may be any that keep to these rules, and one draw needn't show every extreme that they name: `group_adapter_list`: each group's row names 4 different adapters; every adapter is named by some group. `token_adapter_slot`: within each group's 896 rows, a first run of at least 4 segments of 128 rows each holds one slot in a leading run of one or more rows and -1 in the rest; the later segments hold only -1; each slot 0 .. 3 appears in every group.
All inputs are finite; a program needn't handle non-finite values.
Results may differ from a plain program's by a relative error of at most 0.019.
Values may be sent and summed in bfloat16 or wider, within the bound.
A program may use at most 192 MiB of HBM per device.

v0:
```python
import jax
import jax.numpy as jnp
from jax import lax
from jax.sharding import PartitionSpec as P

SEG = 128
USE = 4
STEP = 20


ADAPTER_SCALE = 2.0
LEARN_RATE = 0.001
BETA_ONE = 0.9
BETA_TWO = 0.999
ADAM_EPS = 1e-08


def moment_optimizer_step(param, moment, second, grad):
    new_moment = BETA_ONE * moment + (1.0 - BETA_ONE) * grad
    new_second = BETA_TWO * second + (1.0 - BETA_TWO) * grad * grad
    fix_one = 1.0 - BETA_ONE**STEP
    fix_two = 1.0 - BETA_TWO**STEP
    new_param = param - LEARN_RATE * (new_moment / fix_one) / (
        jnp.sqrt(new_second / fix_two) + ADAM_EPS
    )
    return (new_param, new_moment, new_second)


def per_device(
    hidden,
    frozen_down_matrix,
    cotangent,
    adapter_input_maps,
    adapter_output_maps,
    input_first_moment,
    input_second_moment,
    output_first_moment,
    output_second_moment,
    group_adapter_list,
    token_adapter_slot,
):
    row_number = hidden.shape[0]
    hidden_unit_width = hidden.shape[1]
    model_feature_width = cotangent.shape[1]
    adapter_rank_size = adapter_input_maps.shape[1]
    held_adapters = adapter_input_maps.shape[0]
    group_count = lax.axis_size("grp")
    segment_count = row_number // SEG
    adapter_count = held_adapters * group_count
    token_overall_count = row_number * group_count
    input_map_half, output_map_half = (
        lax.all_gather(adapter_input_maps.astype(jnp.bfloat16), "grp", axis=0, tiled=True),
        lax.all_gather(adapter_output_maps.astype(jnp.bfloat16), "grp", axis=0, tiled=True),
    )
    segment_slot = jnp.maximum(token_adapter_slot.reshape(segment_count, SEG)[:, 0], 0)
    slot_hits = segment_slot[:, None] == jnp.arange(USE)[None, :]
    piece_adapter_index = jnp.sum(jnp.where(slot_hits, group_adapter_list[0][None, :], 0), axis=1)
    valid_mask = (token_adapter_slot >= 0).astype(jnp.float32).reshape(segment_count, SEG, 1)
    input_map_rows = jnp.take(input_map_half, piece_adapter_index, axis=0)
    output_map_rows = jnp.take(output_map_half, piece_adapter_index, axis=0)
    hidden_pieces = hidden.reshape(segment_count, SEG, hidden_unit_width)
    upstream_gradient_pieces = cotangent.reshape(segment_count, SEG, model_feature_width)
    down_part = jnp.einsum(
        "sqf,srf->sqr", hidden_pieces, input_map_rows, preferred_element_type=jnp.float32
    )
    back_part = jnp.einsum(
        "sqd,srd->sqr",
        upstream_gradient_pieces,
        output_map_rows,
        preferred_element_type=jnp.float32,
    )
    rank_total = lax.psum(
        jnp.concatenate([down_part, back_part], axis=2).astype(jnp.bfloat16), "tp"
    ).astype(jnp.float32)
    half_rank_size = (valid_mask * rank_total).astype(jnp.bfloat16)
    adapter_input_product = half_rank_size[:, :, :adapter_rank_size]
    adapter_gradient_path = half_rank_size[:, :, adapter_rank_size:]
    partial_product = jnp.dot(hidden, frozen_down_matrix, preferred_element_type=jnp.float32)
    frozen_output = lax.psum_scatter(
        partial_product.astype(jnp.bfloat16), "tp", scatter_dimension=1, tiled=True
    ).astype(jnp.float32)
    adapter_output_product = jnp.einsum(
        "uxo,uow->uxw", adapter_input_product, output_map_rows, preferred_element_type=jnp.float32
    )
    output = (
        frozen_output
        + ADAPTER_SCALE * adapter_output_product.reshape(row_number, model_feature_width)
    ).astype(jnp.bfloat16)
    frozen_gradient_path = jnp.einsum(
        "td,fd->tf",
        lax.all_gather(cotangent, "tp", axis=1, tiled=True),
        frozen_down_matrix,
        preferred_element_type=jnp.float32,
    )
    adapter_hidden_gradient = jnp.einsum(
        "vjz,vzk->vjk", adapter_gradient_path, input_map_rows, preferred_element_type=jnp.float32
    )
    hidden_gradient = (
        frozen_gradient_path
        + ADAPTER_SCALE * adapter_hidden_gradient.reshape(row_number, hidden_unit_width)
    ).astype(jnp.bfloat16)
    segment_grad_a = jnp.einsum(
        "jxm,jxy->jmy", adapter_gradient_path, hidden_pieces, preferred_element_type=jnp.float32
    )
    segment_grad_b = jnp.einsum(
        "wae,wab->web",
        adapter_input_product,
        upstream_gradient_pieces,
        preferred_element_type=jnp.float32,
    )
    gradient_factor = ADAPTER_SCALE / token_overall_count
    owner_hits = (piece_adapter_index[:, None] == jnp.arange(adapter_count)[None, :]).astype(
        jnp.float32
    )
    input_map_gradient = (
        jnp.einsum("sa,srf->arf", owner_hits, segment_grad_a, precision=lax.Precision.HIGHEST)
        * gradient_factor
    )
    output_map_gradient = (
        jnp.einsum("sa,srd->ard", owner_hits, segment_grad_b, precision=lax.Precision.HIGHEST)
        * gradient_factor
    )
    total_a, total_b = (
        lax.psum(input_map_gradient.astype(jnp.bfloat16), "grp").astype(jnp.float32),
        lax.psum(output_map_gradient.astype(jnp.bfloat16), "grp").astype(jnp.float32),
    )
    first_owned = lax.axis_index("grp") * held_adapters
    held_input_maps = lax.dynamic_slice_in_dim(total_a, first_owned, held_adapters, 0)
    held_output_maps = lax.dynamic_slice_in_dim(total_b, first_owned, held_adapters, 0)
    updated_input_maps, updated_input_first_moment, updated_input_second_moment = (
        moment_optimizer_step(
            adapter_input_maps, input_first_moment, input_second_moment, held_input_maps
        )
    )
    updated_output_maps, updated_output_first_moment, updated_output_second_moment = (
        moment_optimizer_step(
            adapter_output_maps, output_first_moment, output_second_moment, held_output_maps
        )
    )
    return (
        output,
        hidden_gradient,
        updated_input_maps,
        updated_output_maps,
        updated_input_first_moment,
        updated_input_second_moment,
        updated_output_first_moment,
        updated_output_second_moment,
    )


def solution(mesh):
    return jax.shard_map(
        per_device,
        mesh=mesh,
        in_specs=(
            P("grp", "tp"),
            P("tp", None),
            P("grp", "tp"),
            P("grp", None, "tp"),
            P("grp", None, "tp"),
            P("grp", None, "tp"),
            P("grp", None, "tp"),
            P("grp", None, "tp"),
            P("grp", None, "tp"),
            P("grp", None),
            P("grp"),
        ),
        out_specs=(
            P("grp", "tp"),
            P("grp", "tp"),
            P("grp", None, "tp"),
            P("grp", None, "tp"),
            P("grp", None, "tp"),
            P("grp", None, "tp"),
            P("grp", None, "tp"),
            P("grp", None, "tp"),
        ),
        check_vma=False,
    )
```

profile of v0, /device:TPU:1, one launch (start us, length us, event | category | flops | bytes accessed | tf_op | source)
XLA Modules:
  0.0 540.9 jit_solution(14042152267980136502)
XLA Ops:
  7.2 0.0 copy-start
  7.2 0.0 all-gather.6.cloned.1.call-start
  7.2 1.7 convert_element_type.42
  8.9 0.0 all-gather.6.cloned.1.call-update
  8.9 0.0 all-gather.4.cloned.1.call-start
  9.0 1.7 convert_element_type.41
  10.7 0.0 all-gather.4.cloned.1.call-update
  10.8 0.0 all-reduce.4.cloned.1.call-start
  10.8 0.8 maximum_reduce_fusion
  11.6 0.7 select_reduce_fusion
  12.4 0.1 copy.117
  12.4 0.1 fusion.20
  12.6 47.1 %all-gather.6.cloned.1.call-done = bf16[16,64,512]{2,1,0:T(8,128)(2,1)} async-done(((bf16[1,64,512]{2,1,0:T(8,128)(2,1)}), bf16[16,64,512]{2,1,0:T(8,128)(2,1)}) %all-gather.6.cloned.1.call-update) | async-done | bytes 1048592 | tf_op jit(solution)/shard_map/all_gather | solution.py:53
  59.7 2.6 gather_fusion.1
  62.2 1.8 fusion.6
  64.0 50.4 %all-gather.4.cloned.1.call-done = bf16[16,64,1792]{2,1,0:T(8,128)(2,1)} async-done(((bf16[1,64,1792]{2,1,0:T(8,128)(2,1)}), bf16[16,64,1792]{2,1,0:T(8,128)(2,1)}) %all-gather.4.cloned.1.call-update) | async-done | bytes 3670032 | tf_op jit(solution)/shard_map/all_gather | solution.py:52
  114.5 3.9 gather_fusion
  118.3 0.0 copy-done
  118.3 0.0 copy-start.9
  118.3 2.7 fusion.7
  121.0 0.7 pad_maximum_fusion
  121.8 0.0 all-reduce.4.cloned.1.call-update
  121.8 0.0 all-reduce.6.cloned.1.call-start
  121.8 0.0 copy-done.9
  121.8 64.7 %all-reduce.4.cloned.1.call-done = bf16[7,128,128]{1,2,0:T(8,128)(2,1)} async-done(((bf16[7,128,128]{1,2,0:T(8,128)(2,1)}), bf16[7,128,128]{1,2,0:T(8,128)(2,1)}) %all-reduce.4.cloned.1.call-update) | async-done | bytes 229392 | tf_op jit(solution)/shard_map/psum | solution.py:72
  186.5 1.0 multiply_convert_fusion
  187.5 0.0 copy-start.3
  187.5 0.6 fusion.14
  188.1 0.6 copy-done.3
  188.7 0.3 fusion.17
  189.0 5.0 fusion.2
  193.9 6.1 %fusion = bf16[16,64,1792]{2,1,0:T(8,128)(2,1)} fusion(f32[16,64,1792]{2,0,1:T(8,128)S(1)} %fusion.2), kind=kLoop, calls=%fused_computation.3 | loop fusion | flops 3670016 | bytes 11010048 | tf_op jit(solution)/shard_map/convert_element_type | solution.py:124
  200.1 1.6 fusion.8
  201.7 2.4 fusion.4
  204.1 0.0 all-reduce.6.cloned.1.call-update
  204.1 0.0 all-gather.8.cloned.1.call-start
  204.2 0.5 all-gather.8.cloned.1.call-update
  204.7 0.0 reduce-scatter.2.cloned.1.call-start
  204.8 18.6 %convolution_convert_fusion = bf16[896,4096]{1,0:T(8,128)(2,1)} fusion(bf16[896,1792]{1,0:T(8,128)(2,1)S(1)} %copy-done, bf16[1792,4096]{1,0:T(8,128)(2,1)} %param.12), kind=kOutput, calls=%fused_computation.4 | convolution fusion | flops 13157007360 | bytes 25231360 | tf_op jit(solution)/shard_map/dot_general | solution.py:78
  223.3 0.0 copy-start.5
  223.3 0.0 copy-start.2
  223.3 0.0 reduce-scatter.2.cloned.1.call-update
  223.4 1.0 copy-done.5
  224.4 1.8 convolution_multiply_fusion.1
  226.2 0.0 copy-done.2
  226.2 0.0 copy-start.6
  226.2 0.0 copy-start.4
  226.2 0.0 copy-start.7
  226.2 0.0 copy-start.8
  226.2 3.7 convolution_multiply_fusion
  229.8 132.2 %all-reduce.6.cloned.1.call-done = (bf16[16,64,1792]{2,1,0:T(8,128)(2,1)}, bf16[16,64,512]{2,1,0:T(8,128)(2,1)}) async-done(((bf16[16,64,1792]{2,1,0:T(8,128)(2,1)}, bf16[16,64,512]{2,1,0:T(8,128)(2,1)}), (bf16[16,64,1792]{2,1,0:T(8,128)(2,1)}, bf16[16,64,512]{2,1,0:T(8,128)(2,1)})) %all-reduce.6.cloned.1.call-update) | async-done | bytes 4718608 | tf_op jit(solution)/shard_map/psum | solution.py:124
  362.0 0.0 copy-done.6
  362.0 1.8 divide_subtract_fusion.1
  363.8 0.0 copy-done.4
  363.8 0.0 copy-done.7
  363.8 0.0 copy-done.8
  363.8 2.2 divide_subtract_fusion
  366.0 81.1 %all-gather.8.cloned.1.call-done = bf16[896,4096]{1,0:T(8,128)(2,1)} async-done(((bf16[896,512]{1,0:T(8,128)(2,1)}), bf16[896,4096]{1,0:T(8,128)(2,1)}) %all-gather.8.cloned.1.call-update) | async-done | bytes 7340048 | tf_op jit(solution)/shard_map/all_gather | solution.py:91
  447.1 0.0 copy-start.1
  447.1 21.8 %fusion.1 = bf16[896,1792]{1,0:T(8,128)(2,1)} fusion(f32[7,128,1792]{2,1,0:T(8,128)} %convolution_multiply_fusion, bf16[896,4096]{1,0:T(8,128)(2,1)} %all-gather.8.cloned.1.call-done, bf16[1792,4096]{1,0:T(8,128)(2,1)} %param.12), kind=kOutput, calls=%fused_computation.6 | convolution fusion | flops 13156548608 | bytes 31653888 | tf_op jit(solution)/shard_map/td,fd->tf/dot_general | solution.py:89
  468.9 62.2 %reduce-scatter.2.cloned.1.call-done = bf16[896,512]{1,0:T(8,128)(2,1)} async-done(((bf16[896,4096]{1,0:T(8,128)(2,1)}), bf16[896,512]{1,0:T(8,128)(2,1)}) %reduce-scatter.2.cloned.1.call-update) | async-done | bytes 917520 | tf_op jit(solution)/shard_map/reduce_scatter | solution.py:79
  531.1 3.0 fusion.5
  534.1 0.0 copy-done.1
  (3 shorter events, 0.0 us)
Async XLA Ops:
  7.2 111.2 %copy-start = (bf16[896,1792]{1,0:T(8,128)(2,1)S(1)}, bf16[896,1792]{1,0:T(8,128)(2,1)}, u32[]{:S(2)}) copy-start(bf16[896,1792]{1,0:T(8,128)(2,1)} %param.11) | copy-start | bytes 9633796
  7.2 52.5 %all-gather.6.cloned.1.call-start = ((), (), s32[]{:S(2)}) async-start(), calls=%async_computation.3 | async-start | bytes 1114112 | tf_op jit(solution)/shard_map/all_gather | solution.py:53
  8.9 105.5 %all-gather.4.cloned.1.call-start = ((), (), s32[]{:S(2)}) async-start(), calls=%async_computation.2 | async-start | bytes 3899392 | tf_op jit(solution)/shard_map/all_gather | solution.py:52
  10.8 175.8 %all-reduce.4.cloned.1.call-start = ((), (), s32[]{:S(2)}) async-start(), calls=%async_computation.4 | async-start | bytes 458752 | tf_op jit(solution)/shard_map/psum | solution.py:72
  118.3 3.5 copy-start.9
  121.8 240.2 %all-reduce.6.cloned.1.call-start = ((), (), s32[]{:S(2)}) async-start(), calls=%async_computation.6 | async-start | bytes 9437184 | tf_op jit(solution)/shard_map/psum | solution.py:124
  187.5 1.2 copy-start.3
  204.1 242.9 %all-gather.8.cloned.1.call-start = ((), (), s32[]{:S(2)}) async-start(), calls=%async_computation.5 | async-start | bytes 8257536 | tf_op jit(solution)/shard_map/all_gather | solution.py:91
  204.7 326.4 %reduce-scatter.2.cloned.1.call-start = ((), (), s32[]{:S(2)}) async-start(), calls=%async_computation.1 | async-start | bytes 8257536 | tf_op jit(solution)/shard_map/reduce_scatter | solution.py:79
  223.3 1.0 copy-start.5
  223.3 2.8 copy-start.2
  226.2 135.9 %copy-start.6 = (f32[1,64,512]{2,1,0:T(8,128)S(1)}, f32[1,64,512]{2,1,0:T(8,128)}, u32[]{:S(2)}) copy-start(f32[1,64,512]{2,1,0:T(8,128)} %param.15) | copy-start | bytes 393220
  226.2 137.6 %copy-start.4 = (f32[1,64,1792]{2,1,0:T(8,128)S(1)}, f32[1,64,1792]{2,1,0:T(8,128)}, u32[]{:S(2)}) copy-start(f32[1,64,1792]{2,1,0:T(8,128)} %param.14) | copy-start | bytes 1376260
  226.2 137.6 %copy-start.7 = (f32[1,64,1792]{2,1,0:T(8,128)S(1)}, f32[1,64,1792]{2,1,0:T(8,128)}, u32[]{:S(2)}) copy-start(f32[1,64,1792]{2,1,0:T(8,128)} %param.16) | copy-start | bytes 1376260
  226.2 137.6 %copy-start.8 = (f32[1,64,1792]{2,1,0:T(8,128)S(1)}, f32[1,64,1792]{2,1,0:T(8,128)}, u32[]{:S(2)}) copy-start(f32[1,64,1792]{2,1,0:T(8,128)} %param.17) | copy-start | bytes 1376260
  447.1 87.0 %copy-start.1 = (bf16[896,1792]{1,0:T(8,128)(2,1)S(1)}, bf16[896,1792]{1,0:T(8,128)(2,1)}, u32[]{:S(2)}) copy-start(bf16[896,1792]{1,0:T(8,128)(2,1)} %param.11) | copy-start | bytes 9633796
Sparse Core Ops, SparseCore 0:
  11.1 48.5 all-gather.5
  62.7 51.7 all-gather.3
  121.9 64.5 all-reduce.3
  204.2 157.7 all-reduce.5
  363.6 83.4 all-gather.7
  449.5 81.6 reduce-scatter.1
where the time goes:
time: 541 us
  waiting for transfers between devices  438 us (81%)
  matrix products  57.8 us (11%)
  other arithmetic  22.3 us (4%)
  between operations  14.2 us (3%)
  local copies, waits for them, and re-layouts  8.15 us (2%)
    psum x1, waiting for transfers between devices, per_device(): lax.psum(input_map_gradient.astype(jnp.bfloat16), 'grp').astype(jnp.float32)  132 us
    all_gather x1, waiting for transfers between devices, per_device(): lax.all_gather(cotangent, 'tp', axis=1, tiled=True)  81.1 us
    psum x1, waiting for transfers between devices, per_device(): lax.psum(jnp.concatenate([down_part, back_part], axis=2).astype(jnp.bfloa...  64.7 us
    reduce_scatter x1, waiting for transfers between devices, per_device(): lax.psum_scatter(partial_product.astype(jnp.bfloat16), 'tp', scatter_dime...  62.2 us
    all_gather x1, waiting for transfers between devices, per_device(): lax.all_gather(adapter_input_maps.astype(jnp.bfloat16), 'grp', axis=0, ti...  50.4 us
    all_gather x1, waiting for transfers between devices, per_device(): lax.all_gather(adapter_output_maps.astype(jnp.bfloat16), 'grp', axis=0, t...  47.1 us
    dot_general x1, matrix products, per_device(): jnp.einsum('td,fd->tf', lax.all_gather(cotangent, 'tp', axis=1, tiled=Tru...  21.8 us
    dot_general x1, matrix products, per_device(): jnp.dot(hidden, frozen_down_matrix, preferred_element_type=jnp.float32)  18.6 us
  transfers between devices with their start and end apart: 6, of which 6 were waited for; matrix products, arithmetic and copies ran while one was open for 11% of the time, Pallas kernels for 0%

commit v1 on v0

v1 whole, which is shorter than its diff:
```python
import functools

import jax
import jax.numpy as jnp
from jax import lax
from jax.experimental import pallas as pl
from jax.experimental.pallas import tpu as pltpu
from jax.sharding import PartitionSpec as P

MESH = pl.DeviceIdType.MESH
BF = jnp.bfloat16
F32 = jnp.float32

SEG = 128
HALF = 64
SEGS = 7
USE = 4
STEP = 20
RANK = 64
WIDE = USE * RANK
NY = 4
NZ = 4
P_SEGS = (0, 1, 2)
Q_SEGS = (3, 4, 5, 6)
ORDER = (3, 0, 4, 1, 5, 2, 6)

ADAPTER_SCALE = 2.0
LEARN_RATE = 0.001
BETA_ONE = 0.9
BETA_TWO = 0.999
ADAM_EPS = 1e-08


def moment_optimizer_step(param, moment, second, grad):
    new_moment = BETA_ONE * moment + (1.0 - BETA_ONE) * grad
    new_second = BETA_TWO * second + (1.0 - BETA_TWO) * grad * grad
    fix_one = 1.0 - BETA_ONE**STEP
    fix_two = 1.0 - BETA_TWO**STEP
    new_param = param - LEARN_RATE * (new_moment / fix_one) / (
        jnp.sqrt(new_second / fix_two) + ADAM_EPS
    )
    return (new_param, new_moment, new_second)


def nt_dot(a, b):
    return lax.dot_general(a, b, (((1,), (1,)), ((), ())), preferred_element_type=F32)


def tn_dot(a, b):
    return lax.dot_general(a, b, (((0,), (0,)), ((), ())), preferred_element_type=F32)


def nn_dot(a, b):
    return jnp.dot(a, b, preferred_element_type=F32)


G_X, G_U, G_D, G_XU, G_XD, G_O0, G_O1, G_XO0, G_XO1 = range(9)
R_F0, R_F1, R_D0, R_D1, R_U0, R_U1, R_X = range(7)
M_X, M_U, M_D, M_XU, M_XD, M_O, M_XO = range(7)
S_F0, S_F1, S_D0, S_D1, S_U0, S_U1, S_X = range(4, 11)


def kernel(
    grad_scale,
    hid,
    w,
    cot,
    amap,
    bmap,
    lst,
    slots,
    out,
    hgrad,
    gsum,
    wv,
    hv,
    cotf,
    part,
    qf0,
    qf1,
    qru,
    qrd,
    qx,
    pf0,
    pf1,
    pru,
    prd,
    px,
    am32,
    bm32,
    aall,
    acat,
    mask,
    rk,
    rr,
    tot,
    lix,
    lbx,
    gslot,
    con,
    sb,
    gf,
    grd,
    gru,
    gx,
    gtot,
    outv,
    ld_sem,
    w_sem,
    st_sem,
    g_ss,
    g_rs,
    r_ss,
    r_rs,
    k_ss,
    k_rs,
    m_ss,
    m_rs,
    b_ss,
    b_rs,
    s_ss,
    s_rs,
):
    feat = cot.shape[1]
    units = hid.shape[1]
    rows_n = hid.shape[0]
    me = lax.axis_index("tp")
    xl, y = lax.div(me, NY), lax.rem(me, NY)
    ox = 1 - xl
    yu, yd, yo = lax.rem(y + 1, NY), lax.rem(y + 3, NY), lax.rem(y + 2, NY)
    t_x, t_u, t_d, t_o = ox * NY + y, xl * NY + yu, xl * NY + yd, xl * NY + yo
    t_xu, t_xd, t_xo = ox * NY + yu, ox * NY + yd, ox * NY + yo
    g = lax.axis_index("grp")
    xh, z, core = lax.div(g, 2 * NZ), lax.rem(lax.div(g, 2), NZ), lax.rem(g, 2)
    zu, zd, zo = lax.rem(z + 1, NZ), lax.rem(z + 3, NZ), lax.rem(z + 2, NZ)
    oxh = 1 - xh

    def grp_id(a, b, c):
        return a * (2 * NZ) + b * 2 + c

    n_x, n_u, n_d = grp_id(oxh, z, core), grp_id(xh, zu, core), grp_id(xh, zd, core)
    n_s = grp_id(xh, z, 1 - core)

    def col(k):
        return pl.ds(pl.multiple_of(k * feat, 128), feat)

    def seg(s):
        return pl.ds(s * SEG, SEG)

    def half(s, h):
        return pl.ds(s * SEG + h * HALF, HALF)

    ld_a = pltpu.make_async_copy(amap, am32, ld_sem.at[0])
    ld_b = pltpu.make_async_copy(bmap, bm32, ld_sem.at[1])
    ld_h = pltpu.make_async_copy(hid, hv, ld_sem.at[2])
    ld_c = pltpu.make_async_copy(cot, cotf.at[:, col(me)], ld_sem.at[3])
    ld_a.start()
    ld_b.start()
    ld_h.start()
    blocks = [(yq, c) for yq in (yo, yu, yd, y) for c in (0, 1)]
    ld_w = []
    for i, (yq, c) in enumerate(blocks):
        k = c * NY + yq
        ld_w.append(pltpu.make_async_copy(w.at[:, col(k)], wv.at[:, col(k)], w_sem.at[i]))
        ld_w[-1].start()
    ld_c.start()

    barrier = pltpu.get_barrier_semaphore()
    for i in range(1, 2 * NY):
        pl.semaphore_signal(
            barrier, inc=1, device_id={"tp": lax.rem(me + i, 2 * NY)}, device_id_type=MESH
        )
    for dev in (n_x, n_u, n_d, n_s):
        pl.semaphore_signal(barrier, inc=1, device_id={"grp": dev}, device_id_type=MESH)

    ld_a.wait()
    ld_b.wait()
    aall[g, :, pl.ds(0, units)] = am32[...].astype(BF)
    aall[g, :, pl.ds(units, feat)] = bm32[...].astype(BF)

    pl.semaphore_wait(barrier, 2 * NY - 1 + 4)

    sends = []

    def push(src, dst, ss, rs, axis, dev):
        c = pltpu.make_async_remote_copy(
            src_ref=src,
            dst_ref=dst,
            send_sem=ss,
            recv_sem=rs,
            device_id={axis: dev},
            device_id_type=MESH,
        )
        c.start()
        sends.append(c)

    def arrived(dst, ss, rs, axis):
        pltpu.make_async_remote_copy(
            src_ref=dst,
            dst_ref=dst,
            send_sem=ss,
            recv_sem=rs,
            device_id={axis: me if axis == "tp" else g},
            device_id_type=MESH,
        ).wait_recv()

    def g_push(slot, s, rows, k, dev, src=None):
        ref = cotf.at[rows, col(k)]
        push(ref if src is None else src, ref, g_ss.at[slot, s], g_rs.at[slot, s], "tp", dev)

    def g_wait(slot, s, rows, k):
        arrived(cotf.at[rows, col(k)], g_ss.at[slot, s], g_rs.at[slot, s], "tp")

    def gather_start(s):
        own = cot.at[seg(s), :]
        g_push(G_X, s, seg(s), me, t_x, own)
        g_push(G_D, s, seg(s), me, t_u, own)
        g_push(G_U, s, seg(s), me, t_d, own)

    def gather_one(s):
        if s in Q_SEGS:
            g_wait(G_X, s, seg(s), t_x)
            g_push(G_XD, s, seg(s), t_x, t_u)
            g_push(G_XU, s, seg(s), t_x, t_d)
            g_wait(G_D, s, seg(s), t_d)
            g_push(G_O0, s, half(s, 0), t_d, t_u)
            g_wait(G_U, s, seg(s), t_u)
            g_push(G_O1, s, half(s, 1), t_u, t_d)
        else:
            g_wait(G_D, s, seg(s), t_d)
            g_push(G_O0, s, half(s, 0), t_d, t_u)
            g_push(G_XD, s, seg(s), t_d, t_x)
            g_wait(G_U, s, seg(s), t_u)
            g_push(G_O1, s, half(s, 1), t_u, t_d)
            g_push(G_XU, s, seg(s), t_u, t_x)
            g_wait(G_X, s, seg(s), t_x)

    def gather_two(s):
        if s in Q_SEGS:
            g_wait(G_XD, s, seg(s), t_xd)
            g_push(G_XO0, s, half(s, 0), t_xd, t_u)
            g_wait(G_XU, s, seg(s), t_xu)
            g_push(G_XO1, s, half(s, 1), t_xu, t_d)
            g_wait(G_O0, s, half(s, 0), t_o)
            g_wait(G_O1, s, half(s, 1), t_o)
        else:
            g_wait(G_O0, s, half(s, 0), t_o)
            g_push(G_XO0, s, half(s, 0), t_o, t_x)
            g_wait(G_O1, s, half(s, 1), t_o)
            g_push(G_XO1, s, half(s, 1), t_o, t_x)
            g_wait(G_XD, s, seg(s), t_xd)
            g_wait(G_XU, s, seg(s), t_xu)

    def gather_end(s):
        g_wait(G_XO0, s, half(s, 0), t_xo)
        g_wait(G_XO1, s, half(s, 1), t_xo)

    def m_push(slot, o, dev):
        push(aall.at[o], aall.at[o], m_ss.at[slot], m_rs.at[slot], "grp", dev)

    def m_wait(slot, o):
        arrived(aall.at[o], m_ss.at[slot], m_rs.at[slot], "grp")

    def b_push(i, o):
        push(aall.at[o], aall.at[o], b_ss.at[i], b_rs.at[i], "grp", n_s)

    def maps_start():
        m_push(M_X, g, n_x)
        m_push(M_D, g, n_u)
        m_push(M_U, g, n_d)
        b_push(7, g)

    def maps_one():
        m_wait(M_X, n_x)
        m_push(M_XD, n_x, n_u)
        m_push(M_XU, n_x, n_d)
        b_push(M_X, n_x)
        m_wait(M_D, n_d)
        m_push(M_O, n_d, n_u)
        b_push(M_D, n_d)
        m_wait(M_U, n_u)
        b_push(M_U, n_u)

    def maps_two():
        m_wait(M_XU, grp_id(oxh, zu, core))
        m_push(M_XO, grp_id(oxh, zu, core), n_d)
        b_push(M_XU, grp_id(oxh, zu, core))
        m_wait(M_XD, grp_id(oxh, zd, core))
        b_push(M_XD, grp_id(oxh, zd, core))
        m_wait(M_O, grp_id(xh, zo, core))
        b_push(M_O, grp_id(xh, zo, core))

    def maps_end():
        m_wait(M_XO, grp_id(oxh, zo, core))
        b_push(M_XO, grp_id(oxh, zo, core))
        sib = 1 - core
        for i, o in (
            (7, grp_id(xh, z, sib)),
            (M_X, grp_id(oxh, z, sib)),
            (M_D, grp_id(xh, zd, sib)),
            (M_U, grp_id(xh, zu, sib)),
            (M_XU, grp_id(oxh, zu, sib)),
            (M_XD, grp_id(oxh, zd, sib)),
            (M_O, grp_id(xh, zo, sib)),
            (M_XO, grp_id(oxh, zo, sib)),
        ):
            arrived(aall.at[o], b_ss.at[i], b_rs.at[i], "grp")

    def part_block(i):
        yq, c = blocks[i]
        k = c * NY + yq
        ld_w[i].wait()
        step = feat // 2

        @pl.loop(0, 2)
        def _(j):
            wt = wv[:, pl.ds(pl.multiple_of(k * feat + j * step, 128), step)]
            at = pl.ds(pl.multiple_of(c * feat + j * step, 128), step)
            part[yq, :, at] = nn_dot(hv[...], wt).astype(BF)

    def r_push(src, dst, slot, s, dev):
        push(src, dst, r_ss.at[slot, s], r_rs.at[slot, s], "tp", dev)

    def r_wait(dst, slot, s):
        arrived(dst, r_ss.at[slot, s], r_rs.at[slot, s], "tp")

    def bufs(s):
        if s in Q_SEGS:
            i = s - Q_SEGS[0]
            return qf0.at[i], qf1.at[i], qru.at[i], qrd.at[i], pl.ds(0, 2 * feat)
        i = s - P_SEGS[0]
        return pf0.at[i], pf1.at[i], pru.at[i], prd.at[i], col(xl)

    h0, h1 = pl.ds(0, HALF), pl.ds(HALF, HALF)

    def y_sends(s):
        f0, f1, ru, rd, cs = bufs(s)
        r_push(part.at[yo, half(s, 0), cs], f0, R_F0, s, t_u)
        r_push(part.at[yo, half(s, 1), cs], f1, R_F1, s, t_d)
        r_push(part.at[yu, half(s, 1), cs], rd.at[h1, :], R_D1, s, t_u)
        r_push(part.at[yd, half(s, 0), cs], ru.at[h0, :], R_U0, s, t_d)

    def add_into(ref, idx, other):
        ref[idx] = (ref[idx].astype(F32) + other.astype(F32)).astype(BF)

    def scatter_start(s):
        if s in Q_SEGS:
            y_sends(s)
        else:
            r_push(part.at[:, seg(s), col(ox)], px.at[s - P_SEGS[0]], R_X, s, t_x)

    def scatter_x(s):
        i = s - P_SEGS[0]
        r_wait(px.at[i], R_X, s)
        for yq in (yo, yu, yd):
            add_into(part, (yq, seg(s), col(xl)), px[i, yq])
        y_sends(s)

    def scatter_mid(s):
        f0, f1, ru, rd, cs = bufs(s)
        r_wait(f0, R_F0, s)
        add_into(part, (yu, half(s, 0), cs), f0[...])
        r_push(part.at[yu, half(s, 0), cs], rd.at[h0, :], R_D0, s, t_u)
        r_wait(f1, R_F1, s)
        add_into(part, (yd, half(s, 1), cs), f1[...])
        r_push(part.at[yd, half(s, 1), cs], ru.at[h1, :], R_U1, s, t_d)

    def scatter_y(s):
        _, _, ru, rd, _ = bufs(s)
        r_wait(rd.at[h1, :], R_D1, s)
        r_wait(ru.at[h0, :], R_U0, s)
        r_wait(rd.at[h0, :], R_D0, s)
        r_wait(ru.at[h1, :], R_U1, s)
        if s in Q_SEGS:
            i = s - Q_SEGS[0]
            cs = col(ox)
            total = (
                part[y, seg(s), cs].astype(F32)
                + qru[i, :, cs].astype(F32)
                + qrd[i, :, cs].astype(F32)
            )
            part[y, seg(s), cs] = total.astype(BF)
            r_push(part.at[y, seg(s), cs], qx.at[i], R_X, s, t_x)

    def scatter_end(s):
        cs = col(xl)
        if s in Q_SEGS:
            i = s - Q_SEGS[0]
            r_wait(qx.at[i], R_X, s)
            total = (
                part[y, seg(s), cs].astype(F32)
                + qru[i, :, cs].astype(F32)
                + qrd[i, :, cs].astype(F32)
                + qx[i].astype(F32)
            )
        else:
            i = s - P_SEGS[0]
            total = (
                part[y, seg(s), cs].astype(F32)
                + px[i, y].astype(F32)
                + pru[i].astype(F32)
                + prd[i].astype(F32)
            )
        lora = nn_dot(lix[seg(s), :], acat[:, pl.ds(units, feat)])
        outv[seg(s), :] = (total + ADAPTER_SCALE * lora).astype(BF)
        c = pltpu.make_async_copy(outv.at[seg(s), :], out.at[seg(s), :], st_sem.at[s])
        c.start()
        stores.append(c)

    stores = []

    def build_mask():
        lane = lax.broadcasted_iota(jnp.int32, (SEG, WIDE), 1)
        unit = lax.shift_right_logical(lane, 6).astype(F32)
        for s in range(SEGS):
            line = jnp.broadcast_to(slots[pl.ds(s, 1), :].astype(F32), (SEG, SEG))
            wide = jnp.concatenate([line.T] * (WIDE // SEG), axis=1)
            mask[seg(s), :] = jnp.where(wide == unit, 1.0, 0.0).astype(BF)

    def pick(shape, dim, shift):
        i = jnp.bitwise_and(lax.broadcasted_iota(jnp.int32, shape, dim), RANK - 1)
        j = lax.broadcasted_iota(jnp.int32, shape, 1 - dim)
        return jnp.where(i + shift == j, 1.0, 0.0).astype(BF)

    def rank_start():
        for u in range(USE):
            acat[pl.ds(u * RANK, RANK), :] = aall[lst[0, u]]
        m = mask[...].astype(F32)
        down = (nt_dot(hv[...], acat[:, pl.ds(0, units)]) * m).astype(BF)
        back = (nt_dot(cotf[:, col(me)], acat[:, pl.ds(units, feat)]) * m).astype(BF)
        rk[...] = (
            nn_dot(down, pick((WIDE, 2 * RANK), 0, 0))
            + nn_dot(back, pick((WIDE, 2 * RANK), 0, RANK))
        ).astype(BF)
        n = rows_n // (2 * NY)
        for i in range(1, 2 * NY):
            dev = lax.rem(me + i, 2 * NY)
            src = rk.at[pl.ds(pl.multiple_of(dev * n, 16), n), :]
            push(src, rr.at[i], k_ss.at[0, i], k_rs.at[0, i], "tp", dev)

    def rank_sum():
        n = rows_n // (2 * NY)
        mine = pl.ds(pl.multiple_of(me * n, 16), n)
        total = rk[mine, :].astype(F32)
        for i in range(1, 2 * NY):
            arrived(rr.at[i], k_ss.at[0, i], k_rs.at[0, i], "tp")
            total = total + rr[i].astype(F32)
        tot[mine, :] = total.astype(BF)
        for i in range(1, 2 * NY):
            dev = lax.rem(me + i, 2 * NY)
            push(tot.at[mine, :], tot.at[mine, :], k_ss.at[1, i], k_rs.at[1, i], "tp", dev)

    def rank_end():
        n = rows_n // (2 * NY)
        for i in range(1, 2 * NY):
            src = lax.rem(me + 2 * NY - i, 2 * NY)
            theirs = pl.ds(pl.multiple_of(src * n, 16), n)
            arrived(tot.at[theirs, :], k_ss.at[1, i], k_rs.at[1, i], "tp")
        m = mask[...].astype(F32)
        lix[...] = (nn_dot(tot[...], pick((2 * RANK, WIDE), 1, 0)) * m).astype(BF)
        lbx[...] = (nn_dot(tot[...], pick((2 * RANK, WIDE), 1, RANK)) * m).astype(BF)

    def grads():
        step = 256
        wide = units + feat

        @pl.loop(0, units // step)
        def _(j):
            at = pl.ds(pl.multiple_of(j * step, 128), step)
            ga = tn_dot(lbx[...], hv[:, at]) * grad_scale
            for u in range(USE):
                gslot[u, :, at] = ga[u * RANK : (u + 1) * RANK, :].astype(BF)

        gb = tn_dot(lix[...], cotf[:, col(me)]) * grad_scale
        for u in range(USE):
            gslot[u, :, pl.ds(units, feat)] = gb[u * RANK : (u + 1) * RANK, :].astype(BF)
        gslot[USE] = jnp.zeros((RANK, wide), BF)
        for o in range(4 * NZ):
            at = jnp.int32(USE)
            for u in range(USE):
                at = jnp.where(lst[0, u] == o, u, at)
            con[o % 2, (o // 2) % NZ, o // (2 * NZ)] = gslot[at]

    def s_push(src, dst, slot, dev):
        push(src, dst, s_ss.at[slot], s_rs.at[slot], "grp", dev)

    def s_wait(dst, slot):
        arrived(dst, s_ss.at[slot], s_rs.at[slot], "grp")

    def sum_start():
        for i, zq in enumerate((zo, zu, zd, z)):
            s_push(con.at[1 - core, zq], sb.at[zq], i, n_s)

    def sum_one():
        s_wait(sb.at[zo], 0)
        add_into(con, (core, zo), sb[zo])
        s_push(con.at[core, zo, 0], gf.at[0], S_F0, n_u)
        s_push(con.at[core, zo, 1], gf.at[1], S_F1, n_d)
        s_wait(sb.at[zu], 1)
        add_into(con, (core, zu), sb[zu])
        s_push(con.at[core, zu, 1], grd.at[1], S_D1, n_u)
        s_wait(sb.at[zd], 2)
        add_into(con, (core, zd), sb[zd])
        s_push(con.at[core, zd, 0], gru.at[0], S_U0, n_d)
        s_wait(sb.at[z], 3)

    def sum_mid():
        s_wait(gf.at[0], S_F0)
        add_into(con, (core, zu, 0), gf[0])
        s_push(con.at[core, zu, 0], grd.at[0], S_D0, n_u)
        s_wait(gf.at[1], S_F1)
        add_into(con, (core, zd, 1), gf[1])
        s_push(con.at[core, zd, 1], gru.at[1], S_U1, n_d)

    def sum_total(h):
        return (
            con[core, z, h].astype(F32)
            + sb[z, h].astype(F32)
            + grd[h].astype(F32)
            + gru[h].astype(F32)
        )

    def sum_x():
        s_wait(grd.at[1], S_D1)
        s_wait(gru.at[0], S_U0)
        s_wait(grd.at[0], S_D0)
        s_wait(gru.at[1], S_U1)
        con[core, z, oxh] = sum_total(oxh).astype(BF)
        s_push(con.at[core, z, oxh], gx, S_X, n_x)

    def sum_end():
        s_wait(gx, S_X)
        gtot[...] = sum_total(xh) + gx[...].astype(F32)
        c = pltpu.make_async_copy(gtot, gsum, st_sem.at[SEGS])
        c.start()
        stores.append(c)

    step = 256
    tiles = units // step

    def hidden_tile(j):
        at = pl.ds(j * step, step)
        r = nt_dot(cotf[...], wv[at, :]) + ADAPTER_SCALE * nn_dot(lbx[...], acat[:, at])
        hv[:, at] = r.astype(BF)
        c = pltpu.make_async_copy(hv.at[:, at], hgrad.at[:, at], st_sem.at[SEGS + 1 + j])
        c.start()
        stores.append(c)

    maps_start()
    for s in ORDER:
        gather_start(s)
    build_mask()
    ld_h.wait()
    part_block(0)
    part_block(1)
    gather_one(ORDER[0])
    part_block(2)
    gather_one(ORDER[1])
    part_block(3)
    maps_one()
    part_block(4)
    gather_one(ORDER[2])
    gather_two(ORDER[0])
    part_block(5)
    gather_one(ORDER[3])
    gather_two(ORDER[1])
    maps_two()
    part_block(6)
    gather_one(ORDER[4])
    gather_two(ORDER[2])
    part_block(7)
    gather_one(ORDER[5])
    gather_two(ORDER[3])
    maps_end()
    ld_c.wait()
    rank_start()
    gather_one(ORDER[6])
    gather_two(ORDER[4])
    for s in ORDER:
        scatter_start(s)
    gather_two(ORDER[5])
    rank_sum()
    gather_two(ORDER[6])
    for s in P_SEGS:
        scatter_x(s)
    rank_end()
    grads()
    sum_start()
    for s in ORDER:
        gather_end(s)
    scatter_mid(ORDER[0])
    sum_one()
    for i in range(6):
        hidden_tile(i)
        scatter_mid(ORDER[i + 1])
        if i == 3:
            sum_mid()
    hidden_tile(6)
    for s in Q_SEGS:
        scatter_y(s)
    sum_x()
    for s in P_SEGS:
        scatter_y(s)
        scatter_end(s)
    sum_end()
    for s in Q_SEGS:
        scatter_end(s)
    for c in sends:
        c.wait_send()
    for c in stores:
        c.wait()


def fused(hidden, w, cot, amap, bmap, lst, slots, rows_all):
    rows, units = hidden.shape
    feat = cot.shape[1]
    wide = units + feat
    nq, np_ = len(Q_SEGS), len(P_SEGS)
    any_ = pl.BlockSpec(memory_space=pl.ANY)
    dma = pltpu.SemaphoreType.DMA
    v = pltpu.VMEM
    return pl.pallas_call(
        functools.partial(kernel, ADAPTER_SCALE / rows_all),
        out_shape=(
            jax.ShapeDtypeStruct((rows, feat), BF),
            jax.ShapeDtypeStruct((rows, units), BF),
            jax.ShapeDtypeStruct((RANK, wide), F32),
        ),
        in_specs=[any_] * 5
        + [pl.BlockSpec(memory_space=pltpu.SMEM), pl.BlockSpec(memory_space=pltpu.VMEM)],
        out_specs=(any_, any_, any_),
        scratch_shapes=[
            v((units, 2 * NY * feat), BF),
            v((rows, units), BF),
            v((rows, 2 * NY * feat), BF),
            v((NY, rows, 2 * feat), BF),
            v((nq, HALF, 2 * feat), BF),
            v((nq, HALF, 2 * feat), BF),
            v((nq, SEG, 2 * feat), BF),
            v((nq, SEG, 2 * feat), BF),
            v((nq, SEG, feat), BF),
            v((np_, HALF, feat), BF),
            v((np_, HALF, feat), BF),
            v((np_, SEG, feat), BF),
            v((np_, SEG, feat), BF),
            v((np_, NY, SEG, feat), BF),
            v((RANK, units), F32),
            v((RANK, feat), F32),
            v((4 * NZ, RANK, wide), BF),
            v((WIDE, wide), BF),
            v((rows, WIDE), BF),
            v((rows, 2 * RANK), BF),
            v((2 * NY, rows // (2 * NY), 2 * RANK), BF),
            v((rows, 2 * RANK), BF),
            v((rows, WIDE), BF),
            v((rows, WIDE), BF),
            v((USE + 1, RANK, wide), BF),
            v((2, NZ, 2, RANK, wide), BF),
            v((NZ, 2, RANK, wide), BF),
            v((2, RANK, wide), BF),
            v((2, RANK, wide), BF),
            v((2, RANK, wide), BF),
            v((RANK, wide), BF),
            v((RANK, wide), F32),
            v((rows, feat), BF),
            dma((4,)),
            dma((2 * NY,)),
            dma((SEGS + 1 + units // 256,)),
            dma((9, SEGS)),
            dma((9, SEGS)),
            dma((7, SEGS)),
            dma((7, SEGS)),
            dma((2, 2 * NY)),
            dma((2, 2 * NY)),
            dma((7,)),
            dma((7,)),
            dma((8,)),
            dma((8,)),
            dma((11,)),
            dma((11,)),
        ],
        compiler_params=pltpu.CompilerParams(
            collective_id=0,
            has_side_effects=True,
            vmem_limit_bytes=64 * 1024 * 1024,
        ),
    )(hidden, w, cot, amap, bmap, lst, slots)


def per_device(
    hidden,
    frozen_down_matrix,
    cotangent,
    adapter_input_maps,
    adapter_output_maps,
    input_first_moment,
    input_second_moment,
    output_first_moment,
    output_second_moment,
    group_adapter_list,
    token_adapter_slot,
):
    units = hidden.shape[1]
    rows_all = hidden.shape[0] * lax.axis_size("grp")
    output, hidden_gradient, grad = fused(
        hidden,
        frozen_down_matrix,
        cotangent,
        adapter_input_maps[0],
        adapter_output_maps[0],
        group_adapter_list,
        token_adapter_slot.reshape(SEGS, SEG),
        rows_all,
    )
    new_a, new_a_m, new_a_v = moment_optimizer_step(
        adapter_input_maps, input_first_moment, input_second_moment, grad[None, :, :units]
    )
    new_b, new_b_m, new_b_v = moment_optimizer_step(
        adapter_output_maps, output_first_moment, output_second_moment, grad[None, :, units:]
    )
    return (output, hidden_gradient, new_a, new_b, new_a_m, new_a_v, new_b_m, new_b_v)


def solution(mesh):
    return jax.shard_map(
        per_device,
        mesh=mesh,
        in_specs=(
            P("grp", "tp"),
            P("tp", None),
            P("grp", "tp"),
            P("grp", None, "tp"),
            P("grp", None, "tp"),
            P("grp", None, "tp"),
            P("grp", None, "tp"),
            P("grp", None, "tp"),
            P("grp", None, "tp"),
            P("grp", None),
            P("grp"),
        ),
        out_specs=(
            P("grp", "tp"),
            P("grp", "tp"),
            P("grp", None, "tp"),
            P("grp", None, "tp"),
            P("grp", None, "tp"),
            P("grp", None, "tp"),
            P("grp", None, "tp"),
            P("grp", None, "tp"),
        ),
        check_vma=False,
    )
```

time: 541 us -> 168 us (0.31)
  waiting for transfers between devices: 438 us -> 0 us
  Pallas kernels: 0 us -> 160 us
  matrix products: 57.8 us -> 0 us
  other arithmetic: 22.3 us -> 4.7 us
  between operations: 14.2 us -> 0.66 us
  local copies, waits for them, and re-layouts: 8.15 us -> 2.62 us
    psum x2 -> x0, waiting for transfers between devices: 197 us -> none  [the longest x1 132 us: per_device(): lax.psum(input_map_gradient.astype(jnp.bfloat16), 'grp').astype(jnp.float32)]
    all_gather x3 -> x0, waiting for transfers between devices: 179 us -> none  [the longest x1 81.1 us: per_device(): lax.all_gather(cotangent, 'tp', axis=1, tiled=True)]
    pallas_call x0 -> x1, Pallas kernels: none -> 160 us  [fused(): pl.pallas_call(functools.partial(kernel, ADAPTER_SCALE / rows_all), out_s...]
    reduce_scatter x1 -> x0, waiting for transfers between devices: 62.2 us -> none  [per_device(): lax.psum_scatter(partial_product.astype(jnp.bfloat16), 'tp', scatter_dime...]
    dot_general x10 -> x0, matrix products: 57.8 us -> none  [the longest x1 21.8 us: per_device(): jnp.einsum('td,fd->tf', lax.all_gather(cotangent, 'tp', axis=1, tiled=Tru...]
    convert_element_type x6 -> x0, other arithmetic: 15.9 us -> none  [the longest x1 6.14 us: per_device(): input_map_gradient.astype(jnp.bfloat16)]
    gather x2 -> x0, local copies, waits for them, and re-layouts: 6.43 us -> none  [the longest x1 3.86 us: per_device(): input_map_rows = jnp.take(input_map_half, piece_adapter_index, axis=0)]
  transfers between devices with their start and end apart: 6 -> 0, of which waited for: 6 -> 0; matrix products, arithmetic and copies ran while one was open for 11% -> 0% of each run, Pallas kernels for 0% -> 0%
where the time goes in v1:
time: 168 us
  Pallas kernels  160 us (95%)
  other arithmetic  4.7 us (3%)
  local copies, waits for them, and re-layouts  2.62 us (2%)
    pallas_call x1, Pallas kernels, fused(): pl.pallas_call(functools.partial(kernel, ADAPTER_SCALE / rows_all), out_s...  160 us
    sub x2, other arithmetic, moment_optimizer_step(): param - LEARN_RATE * (new_moment / fix_one) / (jnp.sqrt(new_second / fix_...  4.7 us

profile of v1, /device:TPU:1, one launch (start us, length us, event | category | flops | bytes accessed | tf_op | source)
XLA Modules:
  0.0 167.8 jit_solution(4936668574255213716)
XLA Ops:
  0.6 159.9 %shard_map.170 = (bf16[896,512]{1,0:T(8,128)(2,1)}, bf16[896,1792]{1,0:T(8,128)(2,1)}, f32[64,2304]{1,0:T(8,128)}) custom-call(bf16[896,1792]{1,0:T(8,128)(2,1)} %hid.1, bf16[1792,4096]{1,0:T(8,128)(2,1)} %w.1, bf16[896,512]{1,0:T(8,128)(2,1)} %cot.1, f32[64,1792]{1,0:T(8,128)} %bitcast.19, f32[64,512]{1,0:T(8,128)} %bitcast.20, s32[1,4]{1,0:T(1,128)} %lst.1, ...), custom_call_target="tpu_custom_call" | custom-call | tf_op jit(solution)/shard_map/pallas_call | solution.py:622
  160.5 0.0 copy-start.1
  160.5 0.0 copy-start
  160.5 2.8 %divide_subtract_fusion = (f32[1,64,1792]{2,1,0:T(8,128)}, f32[1,64,1792]{2,1,0:T(8,128)}, f32[1,64,1792]{2,1,0:T(8,128)}) fusion(f32[1,64,1792]{2,1,0:T(8,128)} %param.14, f32[64,2304]{1,0:T(8,128)} %get-tuple-element.13, f32[1,64,1792]{2,1,0:T(8,128)} %param.16, f32[1,64,1792]{2,1,0:T(8,128)} %param.17), kind=kLoop, calls=%fused_computation.4 | loop fusion | flops 1376256 | bytes 3211264 | tf_op jit(solution)/shard_map/sub | solution.py:39
  163.4 1.9 %divide_subtract_fusion.1 = (f32[1,64,512]{2,1,0:T(8,128)}, f32[1,64,512]{2,1,0:T(8,128)}, f32[1,64,512]{2,1,0:T(8,128)}) fusion(f32[1,64,512]{2,1,0:T(8,128)} %param.15, f32[64,2304]{1,0:T(8,128)} %get-tuple-element.13, f32[1,64,512]{2,1,0:T(8,128)} %param.18, f32[1,64,512]{2,1,0:T(8,128)} %param.19), kind=kLoop, calls=%fused_computation.9 | loop fusion | flops 393216 | bytes 917504 | tf_op jit(solution)/shard_map/sub | solution.py:39
  165.2 0.0 copy-done.1
  165.2 0.9 copy.21
  166.2 0.0 copy-done
  166.2 1.7 %copy.22 = bf16[896,1792]{1,0:T(8,128)(2,1)} copy(bf16[896,1792]{1,0:T(8,128)(2,1)S(1)} %copy-done) | data formatting | bytes 6422528
Async XLA Ops:
  160.5 4.7 %copy-start.1 = (bf16[896,512]{1,0:T(8,128)(2,1)S(1)}, bf16[896,512]{1,0:T(8,128)(2,1)}, u32[]{:S(2)}) copy-start(bf16[896,512]{1,0:T(8,128)(2,1)} %get-tuple-element.28) | copy-start | bytes 2752516
  160.5 5.6 %copy-start = (bf16[896,1792]{1,0:T(8,128)(2,1)S(1)}, bf16[896,1792]{1,0:T(8,128)(2,1)}, u32[]{:S(2)}) copy-start(bf16[896,1792]{1,0:T(8,128)(2,1)} %get-tuple-element.29) | copy-start | bytes 9633796

commit v2 on v1

--- a/solution.py
+++ b/solution.py
@@ -20,9 +20,45 @@
 WIDE = USE * RANK
 NY = 4
 NZ = 4
-P_SEGS = (0, 1, 2)
-Q_SEGS = (3, 4, 5, 6)
-ORDER = (3, 0, 4, 1, 5, 2, 6)
+Y_FIRST = (0, 1, 2)
+X_SUMS = (0, 1)
+Y_SUMS = tuple(s for s in range(SEGS) if s not in X_SUMS)
+CUT = 3 * SEG
+
+ORDER = (
+    ("gs_x", 5), ("gs_u", 2), ("gs_d", 2), ("m_start",), ("gs_d", 3),
+    ("gs_u", 0), ("gs_x", 4), ("gs_u", 5), ("part", 0), ("gs_x", 3),
+    ("part", 1), ("r_so", 5), ("gs_d", 0), ("gs_x", 1), ("part", 2),
+    ("part", 3), ("r_xu", 1), ("g_d", 2), ("m_d",), ("g_d", 0),
+    ("r_so", 2), ("m_x",), ("gs_u", 3), ("gs_d", 5), ("g_u", 0),
+    ("r_su", 2), ("m_u",), ("gs_d", 1), ("gs_u", 4), ("part", 4),
+    ("part", 5), ("r_sd", 6), ("g_d", 5), ("gs_u", 6), ("gs_u", 1),
+    ("r_m1", 2), ("gs_x", 2), ("g_x", 5), ("m_o",), ("m_xu",),
+    ("m_xd",), ("r_xd", 1), ("gs_x", 0), ("gs_d", 4), ("m_xo",),
+    ("g_x", 4), ("gs_d", 6), ("m_end",), ("rank_start",), ("g_u", 2),
+    ("g_d", 3), ("r_so", 6), ("g_u", 3), ("gs_x", 6), ("rank_sum",),
+    ("g_d", 1), ("g_u", 1), ("g_o0", 0), ("part", 6), ("g_d", 4),
+    ("g_xd", 5), ("g_u", 6), ("part", 7), ("g_o1", 0), ("r_su", 3),
+    ("r_sd", 2), ("g_x", 6), ("g_o0", 1), ("g_o1", 2), ("g_u", 5),
+    ("g_x", 3), ("r_su", 6), ("r_xm", 1), ("r_xo", 1), ("rank_end",),
+    ("grads",), ("sum_start",), ("g_o1", 1), ("g_u", 4), ("r_m1", 6),
+    ("r_xo", 0), ("s_o",), ("r_m0", 6), ("r_m0", 2), ("s_d",),
+    ("g_o0", 2), ("r_so", 3), ("s_u",), ("g_end", 0), ("g_xd", 4),
+    ("g_xu", 5), ("r_so", 4), ("g_xu", 4), ("r_sd", 5), ("g_xu", 3),
+    ("r_ao", 1), ("g_d", 6), ("r_y", 2), ("r_xd", 0), ("g_xu", 6),
+    ("r_m1", 3), ("r_y", 6), ("r_xm", 0), ("g_xd", 6), ("s_m1",),
+    ("s_m0",), ("r_xu", 0), ("g_xd", 3), ("r_m0", 3), ("r_sd", 4),
+    ("r_m0", 5), ("r_sd", 3), ("g_end", 2), ("g_end", 1), ("hidA", 0),
+    ("r_m1", 5), ("hidA", 1), ("hidA", 2), ("r_su", 5), ("hidA", 3),
+    ("r_su", 4), ("hidA", 4), ("r_m0", 4), ("hidA", 5), ("g_end", 3),
+    ("g_end", 6), ("r_m1", 4), ("r_ao", 0), ("g_end", 4), ("s_x",),
+    ("r_ad", 0), ("r_au", 1), ("hidA", 6), ("g_end", 5), ("hidB", 0),
+    ("hidB", 1), ("hidB", 2), ("r_m0", 1), ("r_ad", 1), ("r_m1", 1),
+    ("r_y", 3), ("hidB", 3), ("r_end", 6), ("r_y", 5), ("hidB", 4),
+    ("s_end",), ("r_y", 4), ("r_end", 2), ("r_au", 0), ("r_m0", 0),
+    ("r_m1", 0), ("hidB", 5), ("hidB", 6), ("r_end", 5), ("r_end", 3),
+    ("r_end", 1), ("r_end", 4), ("r_end", 0),
+)
 
 ADAPTER_SCALE = 2.0
 LEARN_RATE = 0.001
@@ -69,11 +105,10 @@
     bmap,
     lst,
     slots,
-    out,
-    hgrad,
-    gsum,
+    outv,
+    hv,
+    gtot,
     wv,
-    hv,
     cotf,
     part,
     qf0,
@@ -103,11 +138,8 @@
     grd,
     gru,
     gx,
-    gtot,
-    outv,
     ld_sem,
     w_sem,
-    st_sem,
     g_ss,
     g_rs,
     r_ss,
@@ -178,6 +210,13 @@
     aall[g, :, pl.ds(0, units)] = am32[...].astype(BF)
     aall[g, :, pl.ds(units, feat)] = bm32[...].astype(BF)
 
+    lane = lax.broadcasted_iota(jnp.int32, (SEG, WIDE), 1)
+    unit = lax.shift_right_logical(lane, 6).astype(F32)
+    for s in range(SEGS):
+        line = jnp.broadcast_to(slots[pl.ds(s, 1), :].astype(F32), (SEG, SEG))
+        wide = jnp.concatenate([line.T] * (WIDE // SEG), axis=1)
+        mask[seg(s), :] = jnp.where(wide == unit, 1.0, 0.0).astype(BF)
+
     pl.semaphore_wait(barrier, 2 * NY - 1 + 4)
 
     sends = []
@@ -211,47 +250,56 @@
     def g_wait(slot, s, rows, k):
         arrived(cotf.at[rows, col(k)], g_ss.at[slot, s], g_rs.at[slot, s], "tp")
 
-    def gather_start(s):
-        own = cot.at[seg(s), :]
-        g_push(G_X, s, seg(s), me, t_x, own)
-        g_push(G_D, s, seg(s), me, t_u, own)
-        g_push(G_U, s, seg(s), me, t_d, own)
-
-    def gather_one(s):
-        if s in Q_SEGS:
+    def gs_x(s):
+        g_push(G_X, s, seg(s), me, t_x, cot.at[seg(s), :])
+
+    def gs_u(s):
+        g_push(G_D, s, seg(s), me, t_u, cot.at[seg(s), :])
+
+    def gs_d(s):
+        g_push(G_U, s, seg(s), me, t_d, cot.at[seg(s), :])
+
+    def g_x(s):
+        g_wait(G_X, s, seg(s), t_x)
+        g_push(G_XD, s, seg(s), t_x, t_u)
+        g_push(G_XU, s, seg(s), t_x, t_d)
+
+    def g_d(s):
+        g_wait(G_D, s, seg(s), t_d)
+        g_push(G_O0, s, half(s, 0), t_d, t_u)
+        if s in Y_FIRST:
+            g_push(G_XD, s, seg(s), t_d, t_x)
+
+    def g_u(s):
+        g_wait(G_U, s, seg(s), t_u)
+        g_push(G_O1, s, half(s, 1), t_u, t_d)
+        if s in Y_FIRST:
+            g_push(G_XU, s, seg(s), t_u, t_x)
+
+    def g_xd(s):
+        g_wait(G_XD, s, seg(s), t_xd)
+        g_push(G_XO0, s, half(s, 0), t_xd, t_u)
+
+    def g_xu(s):
+        g_wait(G_XU, s, seg(s), t_xu)
+        g_push(G_XO1, s, half(s, 1), t_xu, t_d)
+
+    def g_o0(s):
+        g_wait(G_O0, s, half(s, 0), t_o)
+        g_push(G_XO0, s, half(s, 0), t_o, t_x)
+
+    def g_o1(s):
+        g_wait(G_O1, s, half(s, 1), t_o)
+        g_push(G_XO1, s, half(s, 1), t_o, t_x)
+
+    def g_end(s):
+        if s in Y_FIRST:
             g_wait(G_X, s, seg(s), t_x)
-            g_push(G_XD, s, seg(s), t_x, t_u)
-            g_push(G_XU, s, seg(s), t_x, t_d)
-            g_wait(G_D, s, seg(s), t_d)
-            g_push(G_O0, s, half(s, 0), t_d, t_u)
-            g_wait(G_U, s, seg(s), t_u)
-            g_push(G_O1, s, half(s, 1), t_u, t_d)
+            g_wait(G_XD, s, seg(s), t_xd)
+            g_wait(G_XU, s, seg(s), t_xu)
         else:
-            g_wait(G_D, s, seg(s), t_d)
-            g_push(G_O0, s, half(s, 0), t_d, t_u)
-            g_push(G_XD, s, seg(s), t_d, t_x)
-            g_wait(G_U, s, seg(s), t_u)
-            g_push(G_O1, s, half(s, 1), t_u, t_d)
-            g_push(G_XU, s, seg(s), t_u, t_x)
-            g_wait(G_X, s, seg(s), t_x)
-
-    def gather_two(s):
-        if s in Q_SEGS:
-            g_wait(G_XD, s, seg(s), t_xd)
-            g_push(G_XO0, s, half(s, 0), t_xd, t_u)
-            g_wait(G_XU, s, seg(s), t_xu)
-            g_push(G_XO1, s, half(s, 1), t_xu, t_d)
             g_wait(G_O0, s, half(s, 0), t_o)
             g_wait(G_O1, s, half(s, 1), t_o)
-        else:
-            g_wait(G_O0, s, half(s, 0), t_o)
-            g_push(G_XO0, s, half(s, 0), t_o, t_x)
-            g_wait(G_O1, s, half(s, 1), t_o)
-            g_push(G_XO1, s, half(s, 1), t_o, t_x)
-            g_wait(G_XD, s, seg(s), t_xd)
-            g_wait(G_XU, s, seg(s), t_xu)
-
-    def gather_end(s):
         g_wait(G_XO0, s, half(s, 0), t_xo)
         g_wait(G_XO1, s, half(s, 1), t_xo)
 
@@ -264,35 +312,45 @@
     def b_push(i, o):
         push(aall.at[o], aall.at[o], b_ss.at[i], b_rs.at[i], "grp", n_s)
 
-    def maps_start():
+    def m_start():
         m_push(M_X, g, n_x)
         m_push(M_D, g, n_u)
         m_push(M_U, g, n_d)
         b_push(7, g)
 
-    def maps_one():
+    def m_x():
         m_wait(M_X, n_x)
         m_push(M_XD, n_x, n_u)
         m_push(M_XU, n_x, n_d)
         b_push(M_X, n_x)
+
+    def m_d():
         m_wait(M_D, n_d)
         m_push(M_O, n_d, n_u)
         b_push(M_D, n_d)
+
+    def m_u():
         m_wait(M_U, n_u)
         b_push(M_U, n_u)
 
-    def maps_two():
+    def m_xu():
         m_wait(M_XU, grp_id(oxh, zu, core))
         m_push(M_XO, grp_id(oxh, zu, core), n_d)
         b_push(M_XU, grp_id(oxh, zu, core))
+
+    def m_xd():
         m_wait(M_XD, grp_id(oxh, zd, core))
         b_push(M_XD, grp_id(oxh, zd, core))
+
+    def m_o():
         m_wait(M_O, grp_id(xh, zo, core))
         b_push(M_O, grp_id(xh, zo, core))
 
-    def maps_end():
+    def m_xo():
         m_wait(M_XO, grp_id(oxh, zo, core))
         b_push(M_XO, grp_id(oxh, zo, core))
+
+    def m_end():
         sib = 1 - core
         for i, o in (
             (7, grp_id(xh, z, sib)),
@@ -307,6 +365,8 @@
             arrived(aall.at[o], b_ss.at[i], b_rs.at[i], "grp")
 
     def part_block(i):
+        if i == 0:
+            ld_h.wait()
         yq, c = blocks[i]
         k = c * NY + yq
         ld_w[i].wait()
@@ -325,97 +385,95 @@
         arrived(dst, r_ss.at[slot, s], r_rs.at[slot, s], "tp")
 
     def bufs(s):
-        if s in Q_SEGS:
-            i = s - Q_SEGS[0]
+        if s in Y_SUMS:
+            i = Y_SUMS.index(s)
             return qf0.at[i], qf1.at[i], qru.at[i], qrd.at[i], pl.ds(0, 2 * feat)
-        i = s - P_SEGS[0]
+        i = X_SUMS.index(s)
         return pf0.at[i], pf1.at[i], pru.at[i], prd.at[i], col(xl)
 
     h0, h1 = pl.ds(0, HALF), pl.ds(HALF, HALF)
 
-    def y_sends(s):
-        f0, f1, ru, rd, cs = bufs(s)
+    def add_into(ref, idx, other):
+        ref[idx] = (ref[idx].astype(F32) + other.astype(F32)).astype(BF)
+
+    def r_so(s):
+        f0, f1, _, _, cs = bufs(s)
         r_push(part.at[yo, half(s, 0), cs], f0, R_F0, s, t_u)
         r_push(part.at[yo, half(s, 1), cs], f1, R_F1, s, t_d)
+
+    def r_su(s):
+        _, _, _, rd, cs = bufs(s)
         r_push(part.at[yu, half(s, 1), cs], rd.at[h1, :], R_D1, s, t_u)
+
+    def r_sd(s):
+        _, _, ru, _, cs = bufs(s)
         r_push(part.at[yd, half(s, 0), cs], ru.at[h0, :], R_U0, s, t_d)
 
-    def add_into(ref, idx, other):
-        ref[idx] = (ref[idx].astype(F32) + other.astype(F32)).astype(BF)
-
-    def scatter_start(s):
-        if s in Q_SEGS:
-            y_sends(s)
-        else:
-            r_push(part.at[:, seg(s), col(ox)], px.at[s - P_SEGS[0]], R_X, s, t_x)
-
-    def scatter_x(s):
-        i = s - P_SEGS[0]
-        r_wait(px.at[i], R_X, s)
-        for yq in (yo, yu, yd):
-            add_into(part, (yq, seg(s), col(xl)), px[i, yq])
-        y_sends(s)
-
-    def scatter_mid(s):
-        f0, f1, ru, rd, cs = bufs(s)
+    def r_x(j, yq):
+        def send(s):
+            i = X_SUMS.index(s)
+            r_push(part.at[yq, seg(s), col(ox)], px.at[i, j], R_X + j, s, t_x)
+
+        return send
+
+    def r_add(j, yq, after):
+        def add(s):
+            i = X_SUMS.index(s)
+            r_wait(px.at[i, j], R_X + j, s)
+            add_into(part, (yq, seg(s), col(xl)), px[i, j])
+            after(s)
+
+        return add
+
+    def r_m0(s):
+        f0, _, _, rd, cs = bufs(s)
         r_wait(f0, R_F0, s)
         add_into(part, (yu, half(s, 0), cs), f0[...])
         r_push(part.at[yu, half(s, 0), cs], rd.at[h0, :], R_D0, s, t_u)
+
+    def r_m1(s):
+        _, f1, ru, _, cs = bufs(s)
         r_wait(f1, R_F1, s)
         add_into(part, (yd, half(s, 1), cs), f1[...])
         r_push(part.at[yd, half(s, 1), cs], ru.at[h1, :], R_U1, s, t_d)
 
-    def scatter_y(s):
+    def y_wait(s):
         _, _, ru, rd, _ = bufs(s)
+        r_wait(rd.at[h0, :], R_D0, s)
         r_wait(rd.at[h1, :], R_D1, s)
         r_wait(ru.at[h0, :], R_U0, s)
-        r_wait(rd.at[h0, :], R_D0, s)
         r_wait(ru.at[h1, :], R_U1, s)
-        if s in Q_SEGS:
-            i = s - Q_SEGS[0]
-            cs = col(ox)
+
+    def y_total(s, cs):
+        i = Y_SUMS.index(s)
+        return (
+            part[y, seg(s), cs].astype(F32)
+            + qru[i, :, cs].astype(F32)
+            + qrd[i, :, cs].astype(F32)
+        )
+
+    def r_y(s):
+        y_wait(s)
+        part[y, seg(s), col(ox)] = y_total(s, col(ox)).astype(BF)
+        r_push(part.at[y, seg(s), col(ox)], qx.at[Y_SUMS.index(s)], R_X, s, t_x)
+
+    def r_end(s):
+        if s in Y_SUMS:
+            i = Y_SUMS.index(s)
+            r_wait(qx.at[i], R_X, s)
+            total = y_total(s, col(xl)) + qx[i].astype(F32)
+        else:
+            i = X_SUMS.index(s)
+            r_wait(px.at[i, 3], R_X + 3, s)
+            y_wait(s)
             total = (
-                part[y, seg(s), cs].astype(F32)
-                + qru[i, :, cs].astype(F32)
-                + qrd[i, :, cs].astype(F32)
-            )
-            part[y, seg(s), cs] = total.astype(BF)
-            r_push(part.at[y, seg(s), cs], qx.at[i], R_X, s, t_x)
-
-    def scatter_end(s):
-        cs = col(xl)
-        if s in Q_SEGS:
-            i = s - Q_SEGS[0]
-            r_wait(qx.at[i], R_X, s)
-            total = (
-                part[y, seg(s), cs].astype(F32)
-                + qru[i, :, cs].astype(F32)
-                + qrd[i, :, cs].astype(F32)
-                + qx[i].astype(F32)
-            )
-        else:
-            i = s - P_SEGS[0]
-            total = (
-                part[y, seg(s), cs].astype(F32)
-                + px[i, y].astype(F32)
+                part[y, seg(s), col(xl)].astype(F32)
+                + px[i, 3].astype(F32)
                 + pru[i].astype(F32)
                 + prd[i].astype(F32)
             )
         lora = nn_dot(lix[seg(s), :], acat[:, pl.ds(units, feat)])
         outv[seg(s), :] = (total + ADAPTER_SCALE * lora).astype(BF)
-        c = pltpu.make_async_copy(outv.at[seg(s), :], out.at[seg(s), :], st_sem.at[s])
-        c.start()
-        stores.append(c)
-
-    stores = []
-
-    def build_mask():
-        lane = lax.broadcasted_iota(jnp.int32, (SEG, WIDE), 1)
-        unit = lax.shift_right_logical(lane, 6).astype(F32)
-        for s in range(SEGS):
-            line = jnp.broadcast_to(slots[pl.ds(s, 1), :].astype(F32), (SEG, SEG))
-            wide = jnp.concatenate([line.T] * (WIDE // SEG), axis=1)
-            mask[seg(s), :] = jnp.where(wide == unit, 1.0, 0.0).astype(BF)
 
     def pick(shape, dim, shift):
         i = jnp.bitwise_and(lax.broadcasted_iota(jnp.int32, shape, dim), RANK - 1)
@@ -423,6 +481,7 @@
         return jnp.where(i + shift == j, 1.0, 0.0).astype(BF)
 
     def rank_start():
+        ld_c.wait()
         for u in range(USE):
             acat[pl.ds(u * RANK, RANK), :] = aall[lst[0, u]]
         m = mask[...].astype(F32)
@@ -491,23 +550,28 @@
         for i, zq in enumerate((zo, zu, zd, z)):
             s_push(con.at[1 - core, zq], sb.at[zq], i, n_s)
 
-    def sum_one():
+    def s_o():
         s_wait(sb.at[zo], 0)
         add_into(con, (core, zo), sb[zo])
         s_push(con.at[core, zo, 0], gf.at[0], S_F0, n_u)
         s_push(con.at[core, zo, 1], gf.at[1], S_F1, n_d)
+
+    def s_u():
         s_wait(sb.at[zu], 1)
         add_into(con, (core, zu), sb[zu])
         s_push(con.at[core, zu, 1], grd.at[1], S_D1, n_u)
+
+    def s_d():
         s_wait(sb.at[zd], 2)
         add_into(con, (core, zd), sb[zd])
         s_push(con.at[core, zd, 0], gru.at[0], S_U0, n_d)
-        s_wait(sb.at[z], 3)
-
-    def sum_mid():
+
+    def s_m0():
         s_wait(gf.at[0], S_F0)
         add_into(con, (core, zu, 0), gf[0])
         s_push(con.at[core, zu, 0], grd.at[0], S_D0, n_u)
+
+    def s_m1():
         s_wait(gf.at[1], S_F1)
         add_into(con, (core, zd, 1), gf[1])
         s_push(con.at[core, zd, 1], gru.at[1], S_U1, n_d)
@@ -520,7 +584,8 @@
             + gru[h].astype(F32)
         )
 
-    def sum_x():
+    def s_x():
+        s_wait(sb.at[z], 3)
         s_wait(grd.at[1], S_D1)
         s_wait(gru.at[0], S_U0)
         s_wait(grd.at[0], S_D0)
@@ -528,110 +593,98 @@
         con[core, z, oxh] = sum_total(oxh).astype(BF)
         s_push(con.at[core, z, oxh], gx, S_X, n_x)
 
-    def sum_end():
+    def s_end():
         s_wait(gx, S_X)
         gtot[...] = sum_total(xh) + gx[...].astype(F32)
-        c = pltpu.make_async_copy(gtot, gsum, st_sem.at[SEGS])
-        c.start()
-        stores.append(c)
-
-    step = 256
-    tiles = units // step
-
-    def hidden_tile(j):
-        at = pl.ds(j * step, step)
-        r = nt_dot(cotf[...], wv[at, :]) + ADAPTER_SCALE * nn_dot(lbx[...], acat[:, at])
-        hv[:, at] = r.astype(BF)
-        c = pltpu.make_async_copy(hv.at[:, at], hgrad.at[:, at], st_sem.at[SEGS + 1 + j])
-        c.start()
-        stores.append(c)
-
-    maps_start()
-    for s in ORDER:
-        gather_start(s)
-    build_mask()
-    ld_h.wait()
-    part_block(0)
-    part_block(1)
-    gather_one(ORDER[0])
-    part_block(2)
-    gather_one(ORDER[1])
-    part_block(3)
-    maps_one()
-    part_block(4)
-    gather_one(ORDER[2])
-    gather_two(ORDER[0])
-    part_block(5)
-    gather_one(ORDER[3])
-    gather_two(ORDER[1])
-    maps_two()
-    part_block(6)
-    gather_one(ORDER[4])
-    gather_two(ORDER[2])
-    part_block(7)
-    gather_one(ORDER[5])
-    gather_two(ORDER[3])
-    maps_end()
-    ld_c.wait()
-    rank_start()
-    gather_one(ORDER[6])
-    gather_two(ORDER[4])
-    for s in ORDER:
-        scatter_start(s)
-    gather_two(ORDER[5])
-    rank_sum()
-    gather_two(ORDER[6])
-    for s in P_SEGS:
-        scatter_x(s)
-    rank_end()
-    grads()
-    sum_start()
-    for s in ORDER:
-        gather_end(s)
-    scatter_mid(ORDER[0])
-    sum_one()
-    for i in range(6):
-        hidden_tile(i)
-        scatter_mid(ORDER[i + 1])
-        if i == 3:
-            sum_mid()
-    hidden_tile(6)
-    for s in Q_SEGS:
-        scatter_y(s)
-    sum_x()
-    for s in P_SEGS:
-        scatter_y(s)
-        scatter_end(s)
-    sum_end()
-    for s in Q_SEGS:
-        scatter_end(s)
+
+    def hidden_tile(part_no):
+        rows = pl.ds(0, CUT) if part_no == 0 else pl.ds(CUT, rows_n - CUT)
+
+        def tile(j):
+            at = pl.ds(j * 256, 256)
+            r = nt_dot(cotf[rows, :], wv[at, :])
+            r = r + ADAPTER_SCALE * nn_dot(lbx[rows, :], acat[:, at])
+            hv[rows, at] = r.astype(BF)
+
+        return tile
+
+    tasks = dict(
+        gs_x=gs_x,
+        gs_u=gs_u,
+        gs_d=gs_d,
+        g_x=g_x,
+        g_d=g_d,
+        g_u=g_u,
+        g_xd=g_xd,
+        g_xu=g_xu,
+        g_o0=g_o0,
+        g_o1=g_o1,
+        g_end=g_end,
+        m_start=m_start,
+        m_x=m_x,
+        m_d=m_d,
+        m_u=m_u,
+        m_xu=m_xu,
+        m_xd=m_xd,
+        m_o=m_o,
+        m_xo=m_xo,
+        m_end=m_end,
+        part=part_block,
+        r_so=r_so,
+        r_su=r_su,
+        r_sd=r_sd,
+        r_xo=r_x(0, yo),
+        r_xu=r_x(1, yu),
+        r_xd=r_x(2, yd),
+        r_xm=r_x(3, y),
+        r_ao=r_add(0, yo, r_so),
+        r_au=r_add(1, yu, r_su),
+        r_ad=r_add(2, yd, r_sd),
+        r_m0=r_m0,
+        r_m1=r_m1,
+        r_y=r_y,
+        r_end=r_end,
+        rank_start=rank_start,
+        rank_sum=rank_sum,
+        rank_end=rank_end,
+        grads=grads,
+        sum_start=sum_start,
+        s_o=s_o,
+        s_u=s_u,
+        s_d=s_d,
+        s_m0=s_m0,
+        s_m1=s_m1,
+        s_x=s_x,
+        s_end=s_end,
+        hidA=hidden_tile(0),
+        hidB=hidden_tile(1),
+    )
+    for name, *index in ORDER:
+        tasks[name](*index)
     for c in sends:
         c.wait_send()
-    for c in stores:
-        c.wait()
 
 
 def fused(hidden, w, cot, amap, bmap, lst, slots, rows_all):
     rows, units = hidden.shape
     feat = cot.shape[1]
     wide = units + feat
-    nq, np_ = len(Q_SEGS), len(P_SEGS)
+    nq, np_ = len(Y_SUMS), len(X_SUMS)
     any_ = pl.BlockSpec(memory_space=pl.ANY)
     dma = pltpu.SemaphoreType.DMA
     v = pltpu.VMEM
     return pl.pallas_call(
         functools.partial(kernel, ADAPTER_SCALE / rows_all),
         out_shape=(
-            jax.ShapeDtypeStruct((rows, feat), BF),
-            jax.ShapeDtypeStruct((rows, units), BF),
-            jax.ShapeDtypeStruct((RANK, wide), F32),
+            pltpu.VMEM((rows, feat), BF),
+            pltpu.VMEM((rows, units), BF),
+            pltpu.VMEM((RANK, wide), F32),
         ),
         in_specs=[any_] * 5
         + [pl.BlockSpec(memory_space=pltpu.SMEM), pl.BlockSpec(memory_space=pltpu.VMEM)],
-        out_specs=(any_, any_, any_),
+        out_specs=(pl.BlockSpec(memory_space=pltpu.VMEM),) * 3,
         scratch_shapes=[
             v((units, 2 * NY * feat), BF),
-            v((rows, units), BF),
             v((rows, 2 * NY * feat), BF),
             v((NY, rows, 2 * feat), BF),
             v((nq, HALF, 2 * feat), BF),
@@ -661,15 +714,12 @@
             v((2, RANK, wide), BF),
             v((2, RANK, wide), BF),
             v((RANK, wide), BF),
-            v((RANK, wide), F32),
-            v((rows, feat), BF),
             dma((4,)),
             dma((2 * NY,)),
-            dma((SEGS + 1 + units // 256,)),
             dma((9, SEGS)),
             dma((9, SEGS)),
-            dma((7, SEGS)),
-            dma((7, SEGS)),
+            dma((10, SEGS)),
+            dma((10, SEGS)),
             dma((2, 2 * NY)),
             dma((2, 2 * NY)),
             dma((7,)),
@@ -682,7 +732,7 @@
         compiler_params=pltpu.CompilerParams(
             collective_id=0,
             has_side_effects=True,
-            vmem_limit_bytes=64 * 1024 * 1024,
+            vmem_limit_bytes=56 * 1024 * 1024,
         ),
     )(hidden, w, cot, amap, bmap, lst, slots)
 
@@ -700,7 +750,6 @@
     group_adapter_list,
     token_adapter_slot,
 ):
-    units = hidden.shape[1]
     rows_all = hidden.shape[0] * lax.axis_size("grp")
     output, hidden_gradient, grad = fused(
         hidden,
@@ -712,6 +761,7 @@
         token_adapter_slot.reshape(SEGS, SEG),
         rows_all,
     )
+    units = hidden.shape[1]
     new_a, new_a_m, new_a_v = moment_optimizer_step(
         adapter_input_maps, input_first_moment, input_second_moment, grad[None, :, :units]
     )

time: 168 us -> 120 us (0.71)
  Pallas kernels: 160 us -> 114 us
  other arithmetic: 4.7 us -> 2.04 us
    pallas_call x1, Pallas kernels: 160 us -> 114 us  [fused(): pl.pallas_call(functools.partial(kernel, ADAPTER_SCALE / rows_all), out_s...]
    sub x2, other arithmetic: 4.7 us -> 2.04 us  [moment_optimizer_step(): param - LEARN_RATE * (new_moment / fix_one) / (jnp.sqrt(new_second / fix_...]
where the time goes in v2:
time: 120 us
  Pallas kernels  114 us (95%)
  local copies, waits for them, and re-layouts  3.19 us (3%)
  other arithmetic  2.04 us (2%)
    pallas_call x1, Pallas kernels, fused(): pl.pallas_call(functools.partial(kernel, ADAPTER_SCALE / rows_all), out_s...  114 us
    unnamed x14, local copies, waits for them, and re-layouts  3.19 us

profile of v2, /device:TPU:1, one launch (start us, length us, event | category | flops | bytes accessed | tf_op | source)
XLA Modules:
  0.0 120.3 jit_solution(10745230314112317713)
XLA Ops:
  0.6 114.4 %shard_map.170 = (bf16[896,512]{1,0:T(8,128)(2,1)S(1)}, bf16[896,1792]{1,0:T(8,128)(2,1)S(1)}, f32[64,2304]{1,0:T(8,128)S(1)}) custom-call(bf16[896,1792]{1,0:T(8,128)(2,1)} %hid.1, bf16[1792,4096]{1,0:T(8,128)(2,1)} %w.1, bf16[896,512]{1,0:T(8,128)(2,1)} %cot.1, f32[64,1792]{1,0:T(8,128)} %bitcast.19, f32[64,512]{1,0:T(8,128)} %bitcast.20, s32[1,4]{1,0:T(1,128)} %lst.1, ...), custom_call_target="tpu_custom_call" | custom-call | tf_op jit(solution)/shard_map/pallas_call | solution.py:676
  115.1 0.9 copy.21
  116.0 0.0 copy-start
  116.0 0.0 copy-start.2
  116.0 0.0 copy-start.3
  116.0 1.7 %copy.22 = bf16[896,1792]{1,0:T(8,128)(2,1)} copy(bf16[896,1792]{1,0:T(8,128)(2,1)S(1)} %get-tuple-element.21) | data formatting | bytes 6422528
  117.7 0.0 copy-start.1
  117.7 0.0 copy-start.4
  117.7 0.0 copy-start.5
  117.7 0.0 copy-done
  117.7 0.1 copy-done.2
  117.8 0.5 copy-done.3
  118.3 1.2 %divide_subtract_fusion = (f32[1,64,1792]{2,1,0:T(8,128)}, f32[1,64,1792]{2,1,0:T(8,128)}, f32[1,64,1792]{2,1,0:T(8,128)}) fusion(f32[1,64,1792]{2,1,0:T(8,128)S(1)} %copy-done, f32[64,2304]{1,0:T(8,128)S(1)} %get-tuple-element.13, f32[1,64,1792]{2,1,0:T(8,128)S(1)} %copy-done.2, f32[1,64,1792]{2,1,0:T(8,128)S(1)} %copy-done.3), kind=kLoop, calls=%fused_computation.4 | loop fusion | flops 1376256 | bytes 3211264 | tf_op jit(solution)/shard_map/sub | solution.py:75
  119.5 0.0 copy-done.1
  119.5 0.0 copy-done.4
  119.5 0.0 copy-done.5
  119.5 0.8 divide_subtract_fusion.1
Async XLA Ops:
  116.0 1.7 %copy-start = (f32[1,64,1792]{2,1,0:T(8,128)S(1)}, f32[1,64,1792]{2,1,0:T(8,128)}, u32[]{:S(2)}) copy-start(f32[1,64,1792]{2,1,0:T(8,128)} %param.14) | copy-start | bytes 1376260
  116.0 1.8 %copy-start.2 = (f32[1,64,1792]{2,1,0:T(8,128)S(1)}, f32[1,64,1792]{2,1,0:T(8,128)}, u32[]{:S(2)}) copy-start(f32[1,64,1792]{2,1,0:T(8,128)} %param.16) | copy-start | bytes 1376260
  116.0 2.3 %copy-start.3 = (f32[1,64,1792]{2,1,0:T(8,128)S(1)}, f32[1,64,1792]{2,1,0:T(8,128)}, u32[]{:S(2)}) copy-start(f32[1,64,1792]{2,1,0:T(8,128)} %param.17) | copy-start | bytes 1376260
  117.7 1.8 %copy-start.1 = (f32[1,64,512]{2,1,0:T(8,128)S(1)}, f32[1,64,512]{2,1,0:T(8,128)}, u32[]{:S(2)}) copy-start(f32[1,64,512]{2,1,0:T(8,128)} %param.15) | copy-start | bytes 393220
  117.7 1.8 %copy-start.4 = (f32[1,64,512]{2,1,0:T(8,128)S(1)}, f32[1,64,512]{2,1,0:T(8,128)}, u32[]{:S(2)}) copy-start(f32[1,64,512]{2,1,0:T(8,128)} %param.18) | copy-start | bytes 393220
  117.7 1.8 %copy-start.5 = (f32[1,64,512]{2,1,0:T(8,128)S(1)}, f32[1,64,512]{2,1,0:T(8,128)}, u32[]{:S(2)}) copy-start(f32[1,64,512]{2,1,0:T(8,128)} %param.19) | copy-start | bytes 393220

commit v3 on v2

--- a/solution.py
+++ b/solution.py
@@ -20,44 +20,48 @@
 WIDE = USE * RANK
 NY = 4
 NZ = 4
-Y_FIRST = (0, 1, 2)
-X_SUMS = (0, 1)
+Y_FIRST = (5, 6)
+X_SUMS = (0, 1, 2)
 Y_SUMS = tuple(s for s in range(SEGS) if s not in X_SUMS)
 CUT = 3 * SEG
 
 ORDER = (
-    ("gs_x", 5), ("gs_u", 2), ("gs_d", 2), ("m_start",), ("gs_d", 3),
-    ("gs_u", 0), ("gs_x", 4), ("gs_u", 5), ("part", 0), ("gs_x", 3),
-    ("part", 1), ("r_so", 5), ("gs_d", 0), ("gs_x", 1), ("part", 2),
-    ("part", 3), ("r_xu", 1), ("g_d", 2), ("m_d",), ("g_d", 0),
-    ("r_so", 2), ("m_x",), ("gs_u", 3), ("gs_d", 5), ("g_u", 0),
-    ("r_su", 2), ("m_u",), ("gs_d", 1), ("gs_u", 4), ("part", 4),
-    ("part", 5), ("r_sd", 6), ("g_d", 5), ("gs_u", 6), ("gs_u", 1),
-    ("r_m1", 2), ("gs_x", 2), ("g_x", 5), ("m_o",), ("m_xu",),
-    ("m_xd",), ("r_xd", 1), ("gs_x", 0), ("gs_d", 4), ("m_xo",),
-    ("g_x", 4), ("gs_d", 6), ("m_end",), ("rank_start",), ("g_u", 2),
-    ("g_d", 3), ("r_so", 6), ("g_u", 3), ("gs_x", 6), ("rank_sum",),
-    ("g_d", 1), ("g_u", 1), ("g_o0", 0), ("part", 6), ("g_d", 4),
-    ("g_xd", 5), ("g_u", 6), ("part", 7), ("g_o1", 0), ("r_su", 3),
-    ("r_sd", 2), ("g_x", 6), ("g_o0", 1), ("g_o1", 2), ("g_u", 5),
-    ("g_x", 3), ("r_su", 6), ("r_xm", 1), ("r_xo", 1), ("rank_end",),
-    ("grads",), ("sum_start",), ("g_o1", 1), ("g_u", 4), ("r_m1", 6),
-    ("r_xo", 0), ("s_o",), ("r_m0", 6), ("r_m0", 2), ("s_d",),
-    ("g_o0", 2), ("r_so", 3), ("s_u",), ("g_end", 0), ("g_xd", 4),
-    ("g_xu", 5), ("r_so", 4), ("g_xu", 4), ("r_sd", 5), ("g_xu", 3),
-    ("r_ao", 1), ("g_d", 6), ("r_y", 2), ("r_xd", 0), ("g_xu", 6),
-    ("r_m1", 3), ("r_y", 6), ("r_xm", 0), ("g_xd", 6), ("s_m1",),
-    ("s_m0",), ("r_xu", 0), ("g_xd", 3), ("r_m0", 3), ("r_sd", 4),
-    ("r_m0", 5), ("r_sd", 3), ("g_end", 2), ("g_end", 1), ("hidA", 0),
-    ("r_m1", 5), ("hidA", 1), ("hidA", 2), ("r_su", 5), ("hidA", 3),
-    ("r_su", 4), ("hidA", 4), ("r_m0", 4), ("hidA", 5), ("g_end", 3),
-    ("g_end", 6), ("r_m1", 4), ("r_ao", 0), ("g_end", 4), ("s_x",),
-    ("r_ad", 0), ("r_au", 1), ("hidA", 6), ("g_end", 5), ("hidB", 0),
-    ("hidB", 1), ("hidB", 2), ("r_m0", 1), ("r_ad", 1), ("r_m1", 1),
-    ("r_y", 3), ("hidB", 3), ("r_end", 6), ("r_y", 5), ("hidB", 4),
-    ("s_end",), ("r_y", 4), ("r_end", 2), ("r_au", 0), ("r_m0", 0),
-    ("r_m1", 0), ("hidB", 5), ("hidB", 6), ("r_end", 5), ("r_end", 3),
-    ("r_end", 1), ("r_end", 4), ("r_end", 0),
+    ("gs_x", 0), ("gs_u", 3), ("gs_d", 1), ("m_start",), ("gs_d", 4),
+    ("gs_d", 2), ("gs_u", 5), ("gs_x", 3), ("part", 0), ("part", 1),
+    ("r_so", 6), ("r_xo", 2), ("r_xo", 1), ("r_so", 3), ("part", 2),
+    ("gs_u", 1), ("part", 3), ("r_su", 6), ("r_su", 3), ("g_d", 5),
+    ("r_xu", 2), ("m_d",), ("gs_d", 0), ("gs_x", 4), ("m_x",),
+    ("m_u",), ("part", 4), ("gs_d", 5), ("r_so", 5), ("part", 5),
+    ("r_xd", 2), ("r_su", 5), ("g_u", 4), ("part", 6), ("r_xd", 0),
+    ("g_x", 0), ("sent", 13), ("m_xu",), ("r_sd", 6), ("gs_u", 2),
+    ("gs_x", 2), ("g_u", 0), ("part", 7), ("m_xd",), ("r_xm", 0),
+    ("g_d", 1), ("mask",), ("g_u", 1), ("g_u", 2), ("gs_u", 0),
+    ("m_o",), ("r_m1", 5), ("sent", 22), ("m_xo",), ("gs_u", 6),
+    ("sent", 26), ("m_end",), ("rank_start",), ("gs_d", 3), ("gs_x", 1),
+    ("g_o0", 5), ("sent", 37), ("g_x", 2), ("sent", 43), ("rank_x",),
+    ("r_xm", 2), ("g_x", 3), ("sent", 55), ("g_x", 1), ("gs_x", 5),
+    ("rank_sum",), ("g_xu", 2), ("g_u", 5), ("r_xu", 1), ("r_ao", 1),
+    ("g_x", 4), ("g_xd", 2), ("rank_y",), ("g_xu", 0), ("g_xd", 1),
+    ("g_u", 3), ("r_ao", 2), ("gs_d", 6), ("sent", 68), ("g_o1", 5),
+    ("g_xd", 0), ("g_xu", 3), ("gs_x", 6), ("g_d", 6), ("g_d", 2),
+    ("g_xd", 3), ("g_d", 0), ("gs_u", 4), ("r_xd", 1), ("r_xo", 0),
+    ("r_sd", 5), ("r_xm", 1), ("g_xu", 1), ("r_so", 4), ("r_m0", 5),
+    ("sent", 75), ("rank_end",), ("grads",), ("sum_start",), ("sent", 88),
+    ("s_o",), ("g_end", 0), ("g_u", 6), ("r_m1", 3), ("g_xu", 4),
+    ("r_sd", 3), ("s_u",), ("g_xd", 4), ("r_m0", 3), ("g_end", 2),
+    ("r_m1", 6), ("sent", 92), ("g_d", 4), ("r_ad", 1), ("r_m1", 1),
+    ("g_o0", 6), ("g_d", 3), ("r_xu", 0), ("sent", 99), ("g_end", 1),
+    ("r_m0", 6), ("r_ao", 0), ("s_d",), ("r_su", 4), ("hidA", 0),
+    ("hidA", 1), ("hidA", 2), ("hidA", 3), ("r_y", 5), ("g_o1", 6),
+    ("r_au", 2), ("r_m0", 2), ("r_m1", 4), ("r_sd", 4), ("r_ad", 2),
+    ("s_m0",), ("r_m0", 4), ("r_m1", 2), ("s_m1",), ("hidA", 4),
+    ("sent", 115), ("r_au", 0), ("r_y", 3), ("hidA", 5), ("g_end", 4),
+    ("hidA", 6), ("r_au", 1), ("r_m0", 1), ("r_y", 6), ("r_end", 5),
+    ("g_end", 5), ("g_end", 3), ("g_end", 6), ("hidB", 0), ("hidB", 1),
+    ("s_x",), ("hidB", 2), ("hidB", 3), ("r_ad", 0), ("r_m1", 0),
+    ("r_m0", 0), ("hidB", 4), ("r_end", 6), ("sent", 137), ("r_y", 4),
+    ("r_end", 3), ("hidB", 5), ("hidB", 6), ("r_end", 2), ("r_end", 1),
+    ("s_end",), ("sent", 143), ("r_end", 0), ("r_end", 4),
 )
 
 ADAPTER_SCALE = 2.0
@@ -127,6 +131,7 @@
     acat,
     mask,
     rk,
+    kx,
     rr,
     tot,
     lix,
@@ -182,6 +187,12 @@
     def half(s, h):
         return pl.ds(s * SEG + h * HALF, HALF)
 
+    barrier = pltpu.get_barrier_semaphore()
+    for dev in (t_x, t_u, t_d, t_o):
+        pl.semaphore_signal(barrier, inc=1, device_id={"tp": dev}, device_id_type=MESH)
+    for dev in (n_x, n_u, n_d, n_s):
+        pl.semaphore_signal(barrier, inc=1, device_id={"grp": dev}, device_id_type=MESH)
+
     ld_a = pltpu.make_async_copy(amap, am32, ld_sem.at[0])
     ld_b = pltpu.make_async_copy(bmap, bm32, ld_sem.at[1])
     ld_h = pltpu.make_async_copy(hid, hv, ld_sem.at[2])
@@ -197,27 +208,7 @@
         ld_w[-1].start()
     ld_c.start()
 
-    barrier = pltpu.get_barrier_semaphore()
-    for i in range(1, 2 * NY):
-        pl.semaphore_signal(
-            barrier, inc=1, device_id={"tp": lax.rem(me + i, 2 * NY)}, device_id_type=MESH
-        )
-    for dev in (n_x, n_u, n_d, n_s):
-        pl.semaphore_signal(barrier, inc=1, device_id={"grp": dev}, device_id_type=MESH)
-
-    ld_a.wait()
-    ld_b.wait()
-    aall[g, :, pl.ds(0, units)] = am32[...].astype(BF)
-    aall[g, :, pl.ds(units, feat)] = bm32[...].astype(BF)
-
-    lane = lax.broadcasted_iota(jnp.int32, (SEG, WIDE), 1)
-    unit = lax.shift_right_logical(lane, 6).astype(F32)
-    for s in range(SEGS):
-        line = jnp.broadcast_to(slots[pl.ds(s, 1), :].astype(F32), (SEG, SEG))
-        wide = jnp.concatenate([line.T] * (WIDE // SEG), axis=1)
-        mask[seg(s), :] = jnp.where(wide == unit, 1.0, 0.0).astype(BF)
-
-    pl.semaphore_wait(barrier, 2 * NY - 1 + 4)
+    pl.semaphore_wait(barrier, 8)
 
     sends = []
 
@@ -313,6 +304,10 @@
         push(aall.at[o], aall.at[o], b_ss.at[i], b_rs.at[i], "grp", n_s)
 
     def m_start():
+        ld_a.wait()
+        ld_b.wait()
+        aall[g, :, pl.ds(0, units)] = am32[...].astype(BF)
+        aall[g, :, pl.ds(units, feat)] = bm32[...].astype(BF)
         m_push(M_X, g, n_x)
         m_push(M_D, g, n_u)
         m_push(M_U, g, n_d)
@@ -475,6 +470,14 @@
         lora = nn_dot(lix[seg(s), :], acat[:, pl.ds(units, feat)])
         outv[seg(s), :] = (total + ADAPTER_SCALE * lora).astype(BF)
 
+    def build_mask():
+        lane = lax.broadcasted_iota(jnp.int32, (SEG, WIDE), 1)
+        unit = lax.shift_right_logical(lane, 6).astype(F32)
+        for s in range(SEGS):
+            line = jnp.broadcast_to(slots[pl.ds(s, 1), :].astype(F32), (SEG, SEG))
+            wide = jnp.concatenate([line.T] * (WIDE // SEG), axis=1)
+            mask[seg(s), :] = jnp.where(wide == unit, 1.0, 0.0).astype(BF)
+
     def pick(shape, dim, shift):
         i = jnp.bitwise_and(lax.broadcasted_iota(jnp.int32, shape, dim), RANK - 1)
         j = lax.broadcasted_iota(jnp.int32, shape, 1 - dim)
@@ -491,30 +494,40 @@
             nn_dot(down, pick((WIDE, 2 * RANK), 0, 0))
             + nn_dot(back, pick((WIDE, 2 * RANK), 0, RANK))
         ).astype(BF)
+        push(rk.at[k_col(ox), :], kx, k_ss.at[0, 0], k_rs.at[0, 0], "tp", t_x)
+
+    def k_col(c):
+        n = rows_n // 2
+        return pl.ds(pl.multiple_of(c * n, 16), n)
+
+    def k_row(t):
         n = rows_n // (2 * NY)
-        for i in range(1, 2 * NY):
-            dev = lax.rem(me + i, 2 * NY)
-            src = rk.at[pl.ds(pl.multiple_of(dev * n, 16), n), :]
-            push(src, rr.at[i], k_ss.at[0, i], k_rs.at[0, i], "tp", dev)
+        return pl.ds(pl.multiple_of(t * n, 16), n)
+
+    def rank_x():
+        arrived(kx, k_ss.at[0, 0], k_rs.at[0, 0], "tp")
+        add_into(rk, (k_col(xl), slice(None)), kx[...])
+        for i, t in enumerate((t_u, t_d, t_o)):
+            push(rk.at[k_row(t), :], rr.at[i], k_ss.at[1, i], k_rs.at[1, i], "tp", t)
 
     def rank_sum():
-        n = rows_n // (2 * NY)
-        mine = pl.ds(pl.multiple_of(me * n, 16), n)
-        total = rk[mine, :].astype(F32)
-        for i in range(1, 2 * NY):
-            arrived(rr.at[i], k_ss.at[0, i], k_rs.at[0, i], "tp")
+        total = rk[k_row(me), :].astype(F32)
+        for i in range(3):
+            arrived(rr.at[i], k_ss.at[1, i], k_rs.at[1, i], "tp")
             total = total + rr[i].astype(F32)
-        tot[mine, :] = total.astype(BF)
-        for i in range(1, 2 * NY):
-            dev = lax.rem(me + i, 2 * NY)
-            push(tot.at[mine, :], tot.at[mine, :], k_ss.at[1, i], k_rs.at[1, i], "tp", dev)
+        tot[k_row(me), :] = total.astype(BF)
+        mine = tot.at[k_row(me), :]
+        for i, t in enumerate((t_u, t_d, t_o)):
+            push(mine, mine, k_ss.at[2, i], k_rs.at[2, i], "tp", t)
+
+    def rank_y():
+        for i, t in enumerate((t_d, t_u, t_o)):
+            arrived(tot.at[k_row(t), :], k_ss.at[2, i], k_rs.at[2, i], "tp")
+        mine = tot.at[k_col(xl), :]
+        push(mine, mine, k_ss.at[0, 1], k_rs.at[0, 1], "tp", t_x)
 
     def rank_end():
-        n = rows_n // (2 * NY)
-        for i in range(1, 2 * NY):
-            src = lax.rem(me + 2 * NY - i, 2 * NY)
-            theirs = pl.ds(pl.multiple_of(src * n, 16), n)
-            arrived(tot.at[theirs, :], k_ss.at[1, i], k_rs.at[1, i], "tp")
+        arrived(tot.at[k_col(ox), :], k_ss.at[0, 1], k_rs.at[0, 1], "tp")
         m = mask[...].astype(F32)
         lix[...] = (nn_dot(tot[...], pick((2 * RANK, WIDE), 1, 0)) * m).astype(BF)
         lbx[...] = (nn_dot(tot[...], pick((2 * RANK, WIDE), 1, RANK)) * m).astype(BF)
@@ -608,7 +621,14 @@
 
         return tile
 
+    def sent(n):
+        while waited[0] < n:
+            sends[waited[0]].wait_send()
+            waited[0] += 1
+
+    waited = [0]
     tasks = dict(
+        sent=sent,
         gs_x=gs_x,
         gs_u=gs_u,
         gs_d=gs_d,
@@ -629,6 +649,7 @@
         m_o=m_o,
         m_xo=m_xo,
         m_end=m_end,
+        mask=build_mask,
         part=part_block,
         r_so=r_so,
         r_su=r_su,
@@ -645,7 +666,9 @@
         r_y=r_y,
         r_end=r_end,
         rank_start=rank_start,
+        rank_x=rank_x,
         rank_sum=rank_sum,
+        rank_y=rank_y,
         rank_end=rank_end,
         grads=grads,
         sum_start=sum_start,
@@ -661,8 +684,7 @@
     )
     for name, *index in ORDER:
         tasks[name](*index)
-    for c in sends:
-        c.wait_send()
+    sent(len(sends))
 
 
 def fused(hidden, w, cot, amap, bmap, lst, slots, rows_all):
@@ -703,7 +725,8 @@
             v((WIDE, wide), BF),
             v((rows, WIDE), BF),
             v((rows, 2 * RANK), BF),
-            v((2 * NY, rows // (2 * NY), 2 * RANK), BF),
+            v((rows // 2, 2 * RANK), BF),
+            v((3, rows // (2 * NY), 2 * RANK), BF),
             v((rows, 2 * RANK), BF),
             v((rows, WIDE), BF),
             v((rows, WIDE), BF),
@@ -720,8 +743,8 @@
             dma((9, SEGS)),
             dma((10, SEGS)),
             dma((10, SEGS)),
-            dma((2, 2 * NY)),
-            dma((2, 2 * NY)),
+            dma((3, 3)),
+            dma((3, 3)),
             dma((7,)),
             dma((7,)),
             dma((8,)),
@@ -735,6 +758,51 @@
             vmem_limit_bytes=56 * 1024 * 1024,
         ),
     )(hidden, w, cot, amap, bmap, lst, slots)
+
+
+def finish_kernel(gv, *refs):
+    ins, hg_in, out_in = refs[:6], refs[6], refs[7]
+    outs, hg_out, out_out = refs[8:14], refs[14], refs[15]
+    bufs, st_sem, mv_sem = refs[16:22], refs[22], refs[23]
+    moves = [
+        pltpu.make_async_copy(hg_in, hg_out, mv_sem.at[0]),
+        pltpu.make_async_copy(out_in, out_out, mv_sem.at[1]),
+    ]
+    for c in moves:
+        c.start()
+    units, feat = ins[0].shape[1], ins[3].shape[1]
+    step = 256
+    for n, first, size in ((0, 0, units), (3, units, feat)):
+        for j in range(size // step):
+            at = pl.ds(j * step, step)
+            new = moment_optimizer_step(
+                ins[n][:, at], ins[n + 1][:, at], ins[n + 2][:, at], gv[:, pl.ds(first + j * step, step)]
+            )
+            for i in range(3):
+                bufs[n + i][:, at] = new[i]
+                c = pltpu.make_async_copy(
+                    bufs[n + i].at[:, at], outs[n + i].at[:, at], st_sem.at[n + i, j]
+                )
+                c.start()
+                moves.append(c)
+    for c in moves:
+        c.wait()
+
+
+def finish(grad, a, am, av, b, bm, bv, hg, out):
+    hbm = pl.BlockSpec(memory_space=pltpu.HBM)
+    vm = pl.BlockSpec(memory_space=pltpu.VMEM)
+    like = lambda x: jax.ShapeDtypeStruct(x.shape, x.dtype)
+    six = (a, am, av, b, bm, bv)
+    return pl.pallas_call(
+        finish_kernel,
+        out_shape=tuple(like(x) for x in six + (hg, out)),
+        in_specs=[vm] * 9,
+        out_specs=(hbm,) * 8,
+        scratch_shapes=[pltpu.VMEM(x.shape, F32) for x in six]
+        + [pltpu.SemaphoreType.DMA((6, a.shape[1] // 256)), pltpu.SemaphoreType.DMA((2,))],
+        compiler_params=pltpu.CompilerParams(vmem_limit_bytes=8 * 1024 * 1024),
+    )(grad, *six, hg, out)
 
 
 def per_device(
@@ -761,14 +829,27 @@
         token_adapter_slot.reshape(SEGS, SEG),
         rows_all,
     )
-    units = hidden.shape[1]
-    new_a, new_a_m, new_a_v = moment_optimizer_step(
-        adapter_input_maps, input_first_moment, input_second_moment, grad[None, :, :units]
+    new_a, new_a_m, new_a_v, new_b, new_b_m, new_b_v, hidden_gradient, output = finish(
+        grad,
+        adapter_input_maps[0],
+        input_first_moment[0],
+        input_second_moment[0],
+        adapter_output_maps[0],
+        output_first_moment[0],
+        output_second_moment[0],
+        hidden_gradient,
+        output,
     )
-    new_b, new_b_m, new_b_v = moment_optimizer_step(
-        adapter_output_maps, output_first_moment, output_second_moment, grad[None, :, units:]
+    return (
+        output,
+        hidden_gradient,
+        new_a[None],
+        new_b[None],
+        new_a_m[None],
+        new_a_v[None],
+        new_b_m[None],
+        new_b_v[None],
     )
-    return (output, hidden_gradient, new_a, new_b, new_a_m, new_a_v, new_b_m, new_b_v)
 
 
 def solution(mesh):

time: 120 us -> 116 us (0.967)
  local copies, waits for them, and re-layouts: 3.19 us -> 0.03 us
  other arithmetic: 2.04 us -> 0 us
    unnamed x14 -> x12, local copies, waits for them, and re-layouts: 3.19 us -> 0.03 us
    pallas_call x0 -> x1, Pallas kernels: none -> 2.96 us  [finish(): pl.pallas_call(finish_kernel, out_shape=tuple((like(x) for x in six + (hg...]
    pallas_call x1, Pallas kernels: 114 us -> 112 us  [fused(): pl.pallas_call(functools.partial(kernel, ADAPTER_SCALE / rows_all), out_s...]
    sub x2 -> x0, other arithmetic: 2.04 us -> none  [moment_optimizer_step(): param - LEARN_RATE * (new_moment / fix_one) / (jnp.sqrt(new_second / fix_...]
where the time goes in v3:
time: 116 us
  Pallas kernels  115 us (99%)
    pallas_call x1, Pallas kernels, fused(): pl.pallas_call(functools.partial(kernel, ADAPTER_SCALE / rows_all), out_s...  112 us
    pallas_call x1, Pallas kernels, finish(): pl.pallas_call(finish_kernel, out_shape=tuple((like(x) for x in six + (hg...  2.96 us

profile of v3, /device:TPU:1, one launch (start us, length us, event | category | flops | bytes accessed | tf_op | source)
XLA Modules:
  0.0 115.9 jit_solution(9224826711244461449)
XLA Ops:
  0.6 0.0 copy-start
  0.6 0.0 copy-start.1
  0.7 0.0 copy-start.2
  0.7 0.0 copy-start.3
  0.7 0.0 copy-start.4
  0.7 0.0 copy-start.5
  0.7 112.0 %shard_map.170 = (bf16[896,512]{1,0:T(8,128)(2,1)S(1)}, bf16[896,1792]{1,0:T(8,128)(2,1)S(1)}, f32[64,2304]{1,0:T(8,128)S(1)}) custom-call(bf16[896,1792]{1,0:T(8,128)(2,1)} %hid.1, bf16[1792,4096]{1,0:T(8,128)(2,1)} %w.1, bf16[896,512]{1,0:T(8,128)(2,1)} %cot.1, f32[64,1792]{1,0:T(8,128)} %bitcast.13, f32[64,512]{1,0:T(8,128)} %bitcast.15, s32[1,4]{1,0:T(1,128)} %lst.1, ...), custom_call_target="tpu_custom_call" | custom-call | tf_op jit(solution)/shard_map/pallas_call | solution.py:698
  112.7 0.0 copy-done
  112.7 0.0 copy-done.1
  112.7 0.0 copy-done.2
  112.7 0.0 copy-done.3
  112.7 0.0 copy-done.4
  112.7 0.0 copy-done.5
  112.7 3.0 %shard_map.171 = (f32[64,1792]{1,0:T(8,128)}, f32[64,1792]{1,0:T(8,128)}, f32[64,1792]{1,0:T(8,128)}, f32[64,512]{1,0:T(8,128)}, f32[64,512]{1,0:T(8,128)}, /*in...) custom-call(f32[64,2304]{1,0:T(8,128)S(1)} %get-tuple-element.19.gv, f32[64,1792]{1,0:T(8,128)S(1)} %bitcast.14, ...), custom_call_target="tpu_custom_call" | custom-call | tf_op jit(solution)/shard_map/pallas_call | solution.py:797
Async XLA Ops:
  0.6 112.0 %copy-start = (f32[1,64,1792]{2,1,0:T(8,128)S(1)}, f32[1,64,1792]{2,1,0:T(8,128)}, u32[]{:S(2)}) copy-start(f32[1,64,1792]{2,1,0:T(8,128)} %param.14) | copy-start | bytes 1376260
  0.6 112.0 %copy-start.1 = (f32[1,64,512]{2,1,0:T(8,128)S(1)}, f32[1,64,512]{2,1,0:T(8,128)}, u32[]{:S(2)}) copy-start(f32[1,64,512]{2,1,0:T(8,128)} %param.15) | copy-start | bytes 393220
  0.7 112.0 %copy-start.2 = (f32[1,64,1792]{2,1,0:T(8,128)S(1)}, f32[1,64,1792]{2,1,0:T(8,128)}, u32[]{:S(2)}) copy-start(f32[1,64,1792]{2,1,0:T(8,128)} %param.16) | copy-start | bytes 1376260
  0.7 112.0 %copy-start.3 = (f32[1,64,1792]{2,1,0:T(8,128)S(1)}, f32[1,64,1792]{2,1,0:T(8,128)}, u32[]{:S(2)}) copy-start(f32[1,64,1792]{2,1,0:T(8,128)} %param.17) | copy-start | bytes 1376260
  0.7 112.0 %copy-start.4 = (f32[1,64,512]{2,1,0:T(8,128)S(1)}, f32[1,64,512]{2,1,0:T(8,128)}, u32[]{:S(2)}) copy-start(f32[1,64,512]{2,1,0:T(8,128)} %param.18) | copy-start | bytes 393220
  0.7 112.0 %copy-start.5 = (f32[1,64,512]{2,1,0:T(8,128)S(1)}, f32[1,64,512]{2,1,0:T(8,128)}, u32[]{:S(2)}) copy-start(f32[1,64,512]{2,1,0:T(8,128)} %param.19) | copy-start | bytes 393220

commit v4 on v3

--- a/solution.py
+++ b/solution.py
@@ -26,42 +26,42 @@
 CUT = 3 * SEG
 
 ORDER = (
-    ("gs_x", 0), ("gs_u", 3), ("gs_d", 1), ("m_start",), ("gs_d", 4),
-    ("gs_d", 2), ("gs_u", 5), ("gs_x", 3), ("part", 0), ("part", 1),
-    ("r_so", 6), ("r_xo", 2), ("r_xo", 1), ("r_so", 3), ("part", 2),
-    ("gs_u", 1), ("part", 3), ("r_su", 6), ("r_su", 3), ("g_d", 5),
-    ("r_xu", 2), ("m_d",), ("gs_d", 0), ("gs_x", 4), ("m_x",),
-    ("m_u",), ("part", 4), ("gs_d", 5), ("r_so", 5), ("part", 5),
-    ("r_xd", 2), ("r_su", 5), ("g_u", 4), ("part", 6), ("r_xd", 0),
-    ("g_x", 0), ("sent", 13), ("m_xu",), ("r_sd", 6), ("gs_u", 2),
-    ("gs_x", 2), ("g_u", 0), ("part", 7), ("m_xd",), ("r_xm", 0),
-    ("g_d", 1), ("mask",), ("g_u", 1), ("g_u", 2), ("gs_u", 0),
-    ("m_o",), ("r_m1", 5), ("sent", 22), ("m_xo",), ("gs_u", 6),
-    ("sent", 26), ("m_end",), ("rank_start",), ("gs_d", 3), ("gs_x", 1),
-    ("g_o0", 5), ("sent", 37), ("g_x", 2), ("sent", 43), ("rank_x",),
-    ("r_xm", 2), ("g_x", 3), ("sent", 55), ("g_x", 1), ("gs_x", 5),
-    ("rank_sum",), ("g_xu", 2), ("g_u", 5), ("r_xu", 1), ("r_ao", 1),
-    ("g_x", 4), ("g_xd", 2), ("rank_y",), ("g_xu", 0), ("g_xd", 1),
-    ("g_u", 3), ("r_ao", 2), ("gs_d", 6), ("sent", 68), ("g_o1", 5),
-    ("g_xd", 0), ("g_xu", 3), ("gs_x", 6), ("g_d", 6), ("g_d", 2),
-    ("g_xd", 3), ("g_d", 0), ("gs_u", 4), ("r_xd", 1), ("r_xo", 0),
-    ("r_sd", 5), ("r_xm", 1), ("g_xu", 1), ("r_so", 4), ("r_m0", 5),
-    ("sent", 75), ("rank_end",), ("grads",), ("sum_start",), ("sent", 88),
-    ("s_o",), ("g_end", 0), ("g_u", 6), ("r_m1", 3), ("g_xu", 4),
-    ("r_sd", 3), ("s_u",), ("g_xd", 4), ("r_m0", 3), ("g_end", 2),
-    ("r_m1", 6), ("sent", 92), ("g_d", 4), ("r_ad", 1), ("r_m1", 1),
-    ("g_o0", 6), ("g_d", 3), ("r_xu", 0), ("sent", 99), ("g_end", 1),
-    ("r_m0", 6), ("r_ao", 0), ("s_d",), ("r_su", 4), ("hidA", 0),
-    ("hidA", 1), ("hidA", 2), ("hidA", 3), ("r_y", 5), ("g_o1", 6),
-    ("r_au", 2), ("r_m0", 2), ("r_m1", 4), ("r_sd", 4), ("r_ad", 2),
-    ("s_m0",), ("r_m0", 4), ("r_m1", 2), ("s_m1",), ("hidA", 4),
-    ("sent", 115), ("r_au", 0), ("r_y", 3), ("hidA", 5), ("g_end", 4),
-    ("hidA", 6), ("r_au", 1), ("r_m0", 1), ("r_y", 6), ("r_end", 5),
-    ("g_end", 5), ("g_end", 3), ("g_end", 6), ("hidB", 0), ("hidB", 1),
-    ("s_x",), ("hidB", 2), ("hidB", 3), ("r_ad", 0), ("r_m1", 0),
-    ("r_m0", 0), ("hidB", 4), ("r_end", 6), ("sent", 137), ("r_y", 4),
-    ("r_end", 3), ("hidB", 5), ("hidB", 6), ("r_end", 2), ("r_end", 1),
-    ("s_end",), ("sent", 143), ("r_end", 0), ("r_end", 4),
+    ("gs_x", 3), ("gs_d", 3), ("gs_u", 4), ("m_start",), ("gs_d", 5),
+    ("gs_d", 1), ("gs_u", 2), ("gs_u", 0), ("part", 0), ("gs_x", 4),
+    ("g_u", 3), ("part", 1), ("r_xo", 0), ("r_so", 3), ("mask",),
+    ("g_u", 5), ("g_d", 4), ("gs_x", 0), ("gs_u", 6), ("gs_d", 6),
+    ("m_d",), ("gs_d", 0), ("g_d", 0), ("gs_d", 4), ("r_xo", 2),
+    ("m_x",), ("r_so", 4), ("part", 2), ("m_u",), ("part", 3),
+    ("r_xu", 0), ("r_su", 5), ("gs_x", 1), ("r_su", 4), ("r_so", 5),
+    ("sent", 11), ("m_o",), ("m_xu",), ("part", 4), ("part", 5),
+    ("r_sd", 5), ("r_xd", 1), ("gs_x", 6), ("g_x", 4), ("r_xu", 1),
+    ("sent", 19), ("m_xd",), ("gs_u", 5), ("gs_u", 3), ("gs_u", 1),
+    ("r_sd", 4), ("sent", 26), ("r_m1", 5), ("m_xo",), ("sent", 34),
+    ("m_end",), ("rank_start",), ("g_o1", 5), ("g_d", 5), ("g_u", 6),
+    ("gs_x", 2), ("g_d", 6), ("r_ad", 1), ("sent", 45), ("rank_x",),
+    ("g_x", 0), ("sent", 52), ("g_o1", 6), ("g_x", 3), ("part", 6),
+    ("part", 7), ("rank_sum",), ("g_x", 1), ("r_m0", 5), ("g_d", 3),
+    ("gs_d", 2), ("g_u", 4), ("g_u", 0), ("sent", 59), ("g_xu", 3),
+    ("g_xd", 4), ("g_x", 2), ("g_xd", 3), ("g_xu", 4), ("g_xd", 0),
+    ("r_ao", 2), ("g_d", 2), ("r_m1", 3), ("rank_y",), ("g_o0", 6),
+    ("g_d", 1), ("g_xd", 1), ("gs_x", 5), ("r_m1", 4), ("r_su", 3),
+    ("g_o0", 5), ("r_xd", 2), ("r_au", 0), ("r_au", 1), ("r_m0", 4),
+    ("g_xu", 1), ("r_xd", 0), ("r_xu", 2), ("r_xo", 1), ("r_m0", 3),
+    ("r_xm", 1), ("g_xu", 0), ("r_sd", 3), ("g_u", 2), ("r_xm", 0),
+    ("r_y", 5), ("r_xm", 2), ("g_u", 1), ("rank_end",), ("g_end", 6),
+    ("grads",), ("sum_start",), ("g_xd", 2), ("g_end", 5), ("sent", 84),
+    ("g_xu", 2), ("g_end", 4), ("g_end", 3), ("hidB", 0), ("s_o",),
+    ("hidB", 1), ("r_so", 6), ("r_sd", 6), ("s_d",), ("s_u",),
+    ("hidB", 2), ("hidB", 3), ("hidB", 4), ("hidB", 5), ("sent", 101),
+    ("s_m0",), ("r_ao", 0), ("s_m1",), ("hidB", 6), ("r_y", 3),
+    ("g_end", 0), ("r_y", 4), ("r_ao", 1), ("r_su", 6), ("sent", 111),
+    ("g_end", 2), ("r_ad", 2), ("g_end", 1), ("hidA", 0), ("hidA", 1),
+    ("hidA", 2), ("r_m1", 6), ("r_m0", 6), ("r_au", 2), ("sent", 118),
+    ("s_x",), ("r_end", 3), ("r_m1", 2), ("hidA", 3), ("r_m0", 2),
+    ("r_m1", 1), ("r_ad", 0), ("r_m1", 0), ("r_end", 4), ("hidA", 4),
+    ("r_end", 5), ("r_m0", 1), ("r_m0", 0), ("sent", 138), ("r_y", 6),
+    ("hidA", 5), ("hidA", 6), ("sent", 143), ("r_end", 2), ("r_end", 1),
+    ("s_end",), ("r_end", 0), ("r_end", 6),
 )
 
 ADAPTER_SCALE = 2.0

time: 116 us -> 116 us (level)
  no operation moved by 1% of the time
where the time goes in v4:
time: 116 us; the launch traced here: 115 us
  Pallas kernels  114 us (98%)
    pallas_call x1, Pallas kernels, fused(): pl.pallas_call(functools.partial(kernel, ADAPTER_SCALE / rows_all), out_s...  111 us
    pallas_call x1, Pallas kernels, finish(): pl.pallas_call(finish_kernel, out_shape=tuple((like(x) for x in six + (hg...  2.96 us

profile of v4, /device:TPU:1, one launch (start us, length us, event | category | flops | bytes accessed | tf_op | source)
XLA Modules:
  0.0 115.1 jit_solution(3157894928090709585)
XLA Ops:
  0.6 0.0 copy-start
  0.6 0.0 copy-start.1
  0.7 0.0 copy-start.2
  0.7 0.0 copy-start.3
  0.7 0.0 copy-start.4
  0.7 0.0 copy-start.5
  0.7 111.2 %shard_map.170 = (bf16[896,512]{1,0:T(8,128)(2,1)S(1)}, bf16[896,1792]{1,0:T(8,128)(2,1)S(1)}, f32[64,2304]{1,0:T(8,128)S(1)}) custom-call(bf16[896,1792]{1,0:T(8,128)(2,1)} %hid.1, bf16[1792,4096]{1,0:T(8,128)(2,1)} %w.1, bf16[896,512]{1,0:T(8,128)(2,1)} %cot.1, f32[64,1792]{1,0:T(8,128)} %bitcast.13, f32[64,512]{1,0:T(8,128)} %bitcast.15, s32[1,4]{1,0:T(1,128)} %lst.1, ...), custom_call_target="tpu_custom_call" | custom-call | tf_op jit(solution)/shard_map/pallas_call | solution.py:698
  111.9 0.0 copy-done
  111.9 0.0 copy-done.1
  111.9 0.0 copy-done.2
  111.9 0.0 copy-done.3
  111.9 0.0 copy-done.4
  111.9 0.0 copy-done.5
  111.9 3.0 %shard_map.171 = (f32[64,1792]{1,0:T(8,128)}, f32[64,1792]{1,0:T(8,128)}, f32[64,1792]{1,0:T(8,128)}, f32[64,512]{1,0:T(8,128)}, f32[64,512]{1,0:T(8,128)}, /*in...) custom-call(f32[64,2304]{1,0:T(8,128)S(1)} %get-tuple-element.19.gv, f32[64,1792]{1,0:T(8,128)S(1)} %bitcast.14, ...), custom_call_target="tpu_custom_call" | custom-call | tf_op jit(solution)/shard_map/pallas_call | solution.py:797
Async XLA Ops:
  0.6 111.2 %copy-start = (f32[1,64,1792]{2,1,0:T(8,128)S(1)}, f32[1,64,1792]{2,1,0:T(8,128)}, u32[]{:S(2)}) copy-start(f32[1,64,1792]{2,1,0:T(8,128)} %param.14) | copy-start | bytes 1376260
  0.6 111.2 %copy-start.1 = (f32[1,64,512]{2,1,0:T(8,128)S(1)}, f32[1,64,512]{2,1,0:T(8,128)}, u32[]{:S(2)}) copy-start(f32[1,64,512]{2,1,0:T(8,128)} %param.15) | copy-start | bytes 393220
  0.7 111.2 %copy-start.2 = (f32[1,64,1792]{2,1,0:T(8,128)S(1)}, f32[1,64,1792]{2,1,0:T(8,128)}, u32[]{:S(2)}) copy-start(f32[1,64,1792]{2,1,0:T(8,128)} %param.16) | copy-start | bytes 1376260
  0.7 111.2 %copy-start.3 = (f32[1,64,1792]{2,1,0:T(8,128)S(1)}, f32[1,64,1792]{2,1,0:T(8,128)}, u32[]{:S(2)}) copy-start(f32[1,64,1792]{2,1,0:T(8,128)} %param.17) | copy-start | bytes 1376260
  0.7 111.2 %copy-start.4 = (f32[1,64,512]{2,1,0:T(8,128)S(1)}, f32[1,64,512]{2,1,0:T(8,128)}, u32[]{:S(2)}) copy-start(f32[1,64,512]{2,1,0:T(8,128)} %param.18) | copy-start | bytes 393220
  0.7 111.2 %copy-start.5 = (f32[1,64,512]{2,1,0:T(8,128)S(1)}, f32[1,64,512]{2,1,0:T(8,128)}, u32[]{:S(2)}) copy-start(f32[1,64,512]{2,1,0:T(8,128)} %param.19) | copy-start | bytes 393220
